TPU v7x, 128 devices: a whole 4x4x4 slice. The times are simulated.
128 devices in a mesh: member: 64 (over z, y, x), region: 2 (over core).
Axes of the slice: x: 4, y: 4, z: 4, core: 2. Of those that a mesh axis runs over, the one named last changes fastest.
Arguments:
- prior_samples: float32 [1024, 64, 2, 1024], P('member', None, 'region'), may hold values from -6 to 6
- measured_point: int32 [64, 2, 256], P('member', 'region'), may hold values from 0 to 1023
- measured_reading: float32 [64, 2, 256], P('member', 'region'), may hold values from -6 to 6
- measurement_noise: bfloat16 [64, 2, 256, 1024], P('member', 'region'), may hold values from -6 to 6
- noise_kind: int32 [64, 2], P('member'), may hold values from 0 to 3
- taper_set: int32 [64, 2], P('member'), may hold values from 0 to 1, as said below
Outputs:
- increment: float32 [1024, 64, 2, 1024], P('member', None, 'region')
Inputs may be any that keep to these rules, and one draw needn't show every extreme that they name: `taper_set`: along the 2 regions of a band the labels never fall, so that equal labels form runs of neighbouring regions; each label is the index of the first region of its run; in at least one band all regions form a single run.
All inputs are finite; a program needn't handle non-finite values.
Results may differ from a plain program's by a relative error of at most 0.0076.
Values may be sent and summed in bfloat16 or wider, within the bound.
No kernel may reach another device: no remote copies, remote signals or barrier semaphores. Data moves between devices by JAX's collectives and lax.ppermute only.
A program may use at most 64 MiB of HBM per device.

v0:
```python
import jax
import jax.numpy as jnp
from jax import lax
from jax.sharding import PartitionSpec as P

ITERS = 4


taper_base = 0.7


def region_weights(groups):
    count = groups.shape[0]
    places = jnp.arange(count, dtype=jnp.int32)
    distance = jnp.abs(places[:, None] - places[None, :]).astype(jnp.float32)
    kept = groups[:, None] == groups[None, :]
    return jnp.where(kept, jnp.power(jnp.float32(taper_base), distance), jnp.float32(0.0))


def cluster_bounds(groups):
    count = groups.shape[0]
    places = jnp.arange(count, dtype=jnp.int32)
    kept = groups[:, None] == groups[None, :]
    starts = jnp.min(jnp.where(kept, places[None, :], count), axis=1)
    finish = jnp.max(jnp.where(kept, places[None, :] + 1, 0), axis=1)
    return (starts, finish)


def pick_entry(values, position):
    places = jnp.arange(values.shape[0], dtype=jnp.int32)
    return jnp.sum(jnp.where(places == position, values, jnp.zeros_like(values)))


def pick_row(matrix, position):
    places = jnp.arange(matrix.shape[0], dtype=jnp.int32)
    return jnp.sum(jnp.where((places == position)[:, None], matrix, jnp.zeros_like(matrix)), axis=0)


def chebyshev(innovation, apply_operator, lowest, highest):
    center = 0.5 * (highest + lowest)
    radius = 0.5 * (highest - lowest)
    sigma_value = center / radius
    rho_value = 1.0 / sigma_value
    residual = innovation
    direction = residual / center
    solution = jnp.zeros_like(innovation)
    for sweep_index in range(ITERS):
        solution = solution + direction
        if sweep_index + 1 < ITERS:
            residual = residual - apply_operator(direction)
            rho_next = 1.0 / (2.0 * sigma_value - rho_value)
            direction = rho_next * rho_value * direction + 2.0 * rho_next / radius * residual
            rho_value = rho_next
    return solution


def shards(
    prior_samples, measured_point, measured_reading, measurement_noise, noise_kind, taper_set
):
    stripe_slice = lax.all_to_all(prior_samples, "member", split_axis=1, concat_axis=0, tiled=True)
    sample_fields = stripe_slice.shape[0]
    cell_count = stripe_slice.shape[3]
    field = stripe_slice.reshape(sample_fields, cell_count)
    sample_mean_state = jnp.mean(field, axis=0)
    sample_deviation = (field - sample_mean_state).astype(jnp.bfloat16)
    positions = measured_point.reshape(-1)
    tile_size = positions.shape[0]
    measured_fields = jnp.take(field, positions, axis=1)
    obs_rows = (measured_fields - sample_mean_state[positions][None, :]).T.astype(jnp.bfloat16)
    regions = lax.axis_size("region")
    region = lax.axis_index("region")
    classes = noise_kind.reshape(-1)
    groups = taper_set.reshape(-1)
    variance_all = 0.5 * jnp.exp2(classes.astype(jnp.float32))
    variance = pick_entry(variance_all, region)
    innovation = (
        measured_reading.reshape(-1)[:, None]
        + jnp.sqrt(variance)
        * measurement_noise.reshape(tile_size, sample_fields).astype(jnp.float32)
        - measured_fields.T
    )
    weights = region_weights(groups)
    my_weights = pick_row(weights, region)
    starts, finish = cluster_bounds(groups)
    first_block = pick_entry(starts, region)
    last_block = pick_entry(finish, region)
    scale_count = sample_fields - 1
    all_rows = lax.all_gather(obs_rows, "region", axis=0, tiled=True)

    def cov_tile(column_block, covered):
        tile_rows = lax.dynamic_slice_in_dim(all_rows, column_block * tile_size, tile_size, 0)
        product = lax.dot_general(
            obs_rows, tile_rows, (((1,), (1,)), ((), ())), preferred_element_type=jnp.float32
        )
        scaled = (pick_entry(my_weights, column_block) * product / scale_count).astype(jnp.bfloat16)
        return lax.dynamic_update_slice_in_dim(covered, scaled, column_block * tile_size, 1)

    cov_row = lax.fori_loop(
        first_block, last_block, cov_tile, jnp.zeros((tile_size, regions * tile_size), jnp.bfloat16)
    )
    upper = variance + jnp.sum(jnp.abs(cov_row.astype(jnp.float32)), axis=1)
    largest = lax.pmax(jnp.max(upper), "region")
    lowest = 0.5 * jnp.exp2(jnp.min(classes).astype(jnp.float32))
    highest = lowest + largest

    def apply_rows(direction):
        gathered = lax.all_gather(direction.astype(jnp.bfloat16), "region", axis=0, tiled=True)

        def add_tile(column_block, total):
            weights_tile = lax.dynamic_slice_in_dim(cov_row, column_block * tile_size, tile_size, 1)
            source_rows = lax.dynamic_slice_in_dim(gathered, column_block * tile_size, tile_size, 0)
            return total + jnp.dot(weights_tile, source_rows, preferred_element_type=jnp.float32)

        summed = lax.fori_loop(
            first_block, last_block, add_tile, jnp.zeros((tile_size, sample_fields), jnp.float32)
        )
        return variance * direction + summed

    local_solution = chebyshev(innovation, apply_rows, lowest, highest)
    solution = lax.all_gather(local_solution.astype(jnp.bfloat16), "region", axis=0, tiled=True)

    def add_gain(column_block, total):
        source_rows = lax.dynamic_slice_in_dim(all_rows, column_block * tile_size, tile_size, 0)
        cross = lax.dot_general(
            sample_deviation,
            source_rows,
            (((0,), (1,)), ((), ())),
            preferred_element_type=jnp.float32,
        )
        gain = (pick_entry(my_weights, column_block) * cross / scale_count).astype(jnp.bfloat16)
        solved_rows = lax.dynamic_slice_in_dim(solution, column_block * tile_size, tile_size, 0)
        return total + lax.dot_general(
            solved_rows, gain, (((0,), (1,)), ((), ())), preferred_element_type=jnp.float32
        )

    increment = lax.fori_loop(
        first_block, last_block, add_gain, jnp.zeros((sample_fields, cell_count), jnp.float32)
    )
    return lax.all_to_all(
        increment.reshape(sample_fields, 1, 1, cell_count).astype(jnp.bfloat16),
        "member",
        split_axis=0,
        concat_axis=1,
        tiled=True,
    ).astype(jnp.float32)


def solution(mesh):
    return jax.shard_map(
        shards,
        mesh=mesh,
        in_specs=(
            P("member", None, "region", None),
            P("member", "region", None),
            P("member", "region", None),
            P("member", "region", None, None),
            P("member", None),
            P("member", None),
        ),
        out_specs=P("member", None, "region", None),
        check_vma=False,
    )
```

profile of v0, /device:TPU:0, one launch (start us, length us, event | category | flops | bytes accessed | tf_op | source)
XLA Modules:
  0.0 293.1 jit_solution(13180317984968135843)
XLA Ops:
  6.5 6.6 %copy.33 = f32[16,64,1,1024]{3,0,2,1:T(8,128)} copy(f32[16,64,1,1024]{3,2,1,0:T(1,128)} %param.16) | data formatting | bytes 8388608 | tf_op args[0]
  13.2 11.9 %all-to-all-start = ((f32[16,64,1,1024]{3,0,2,1:T(8,128)}), f32[16,64,1,1024]{3,0,2,1:T(8,128)}, u32[]{:S(2)}, u32[]{:S(2)}) async-start(f32[16,64,1,1024]{3,0,2,1:T(8,128)} %copy.33), calls=%async_computation | async-start | bytes 8388608 | tf_op jit(solution)/shard_map/all_to_all | solution.py:60
  25.2 54.6 %all-to-all-done = f32[16,64,1,1024]{3,0,2,1:T(8,128)} async-done(((f32[16,64,1,1024]{3,0,2,1:T(8,128)}), f32[16,64,1,1024]{3,0,2,1:T(8,128)}, u32[]{:S(2)}, u32[]{:S(2)}) %all-to-all-start) | async-done | bytes 4194336 | tf_op jit(solution)/shard_map/all_to_all | solution.py:60
  79.8 5.3 %copy.34 = f32[1024,1024]{0,1:T(8,128)} copy(f32[1024,1024]{1,0:T(8,128)} %bitcast.8) | data formatting | bytes 8388608 | tf_op jit(solution)/shard_map/reshape | solution.py:63
  85.1 2.5 reduce_sum.76
  87.6 3.8 %gather_fusion = f32[256,1024]{1,0:T(8,128)S(1)} fusion(f32[1024,1024]{0,1:T(8,128)} %copy.34, s32[1024]{0:T(1024)S(1)} %pad_clamp_fusion), kind=kCustom, calls=%fused_computation | custom fusion | bytes 2098176 | tf_op jit(solution)/shard_map/jit(_take)/gather | solution.py:68
  98.0 6.0 %all-gather.6.cloned.1.call-done = bf16[512,1024]{1,0:T(8,128)(2,1)} async-done(((bf16[256,1024]{1,0:T(8,128)(2,1)}), bf16[512,1024]{1,0:T(8,128)(2,1)}) %all-gather.6.cloned.1.call-update) | async-done | bytes 1048592 | tf_op jit(solution)/shard_map/all_gather | solution.py:88
  104.0 7.5 %while.50 = (s32[]{:T(128)}, bf16[256,512]{0,1:T(8,128)(2,1)S(1)}, s32[]{:T(128)}, f32[2]{0:T(128)S(1)}, bf16[512,1024]{1,0:T(8,128)(2,1)}, /*index=5*/bf16[256,...) while((s32[]{:T(128)}, bf16[256,512]{0,1:T(8,128)(2,1)S(1)}, s32[]{:T(128)}, ...), condition=%wide.region_10.11_spmd, body=%wide.region_8.10_spmd.sunk | while | flops 134414352 | bytes 1181347 | solution.py:98
  105.3 2.1 fusion.56
  108.8 2.1 fusion.56
  112.9 3.1 %pmax.7 = f32[]{:T(128)} all-reduce(f32[]{:T(128)} %add_reduce_fusion), channel_id=1, replica_groups=mesh['member'=64,'region'=2] {'region'}, use_global_device_ids=true, to_apply=%region_13.14 | all-reduce | flops 1 | bytes 8 | tf_op jit(solution)/shard_map/pmax | solution.py:102
  118.7 12.1 %all-gather.8.cloned.1.call-done = bf16[512,1024]{1,0:T(8,128)(2,1)} async-done(((bf16[256,1024]{1,0:T(8,128)(2,1)}), bf16[512,1024]{1,0:T(8,128)(2,1)}) %all-gather.8.cloned.1.call-update) | async-done | bytes 1048592 | tf_op jit(solution)/shard_map/all_gather | solution.py:107
  130.9 4.9 %while.51 = (s32[]{:T(128)}, f32[256,1024]{1,0:T(8,128)S(1)}, s32[]{:T(128)}, bf16[256,512]{1,0:T(8,128)(2,1)S(1)}, bf16[512,1024]{1,0:T(8,128)(2,1)}, /*index=5*/s32[]{:T(128)}, s32[]{:T(128)}, s32[]{:T(128)}, s32[]{:T(128)}) while((s32[]{:T(128)}, f32[256,1024]{1,0:T(8,128)S(1)}, s32[]{:T(128)}, bf16[256,512]{1,0:T(8,128)(2,1)S(1)}, ...), condition=%wide.region_15.16_spmd, body=%wide.region_14.15_spmd.sunk | while | flops 134479872 | bytes 2753675 | solution.py:114
  138.5 12.3 %all-gather.10.cloned.1.call-done = bf16[512,1024]{1,0:T(8,128)(2,1)} async-done(((bf16[256,1024]{1,0:T(8,128)(2,1)}), bf16[512,1024]{1,0:T(8,128)(2,1)}) %all-gather.10.cloned.1.call-update) | async-done | bytes 1048592 | tf_op jit(solution)/shard_map/all_gather | solution.py:107
  150.9 4.9 %while.52 = (s32[]{:T(128)}, f32[256,1024]{1,0:T(8,128)S(1)}, s32[]{:T(128)}, bf16[256,512]{1,0:T(8,128)(2,1)S(1)}, bf16[512,1024]{1,0:T(8,128)(2,1)}, /*index=5*/s32[]{:T(128)}, s32[]{:T(128)}, s32[]{:T(128)}, s32[]{:T(128)}) while((s32[]{:T(128)}, f32[256,1024]{1,0:T(8,128)S(1)}, s32[]{:T(128)}, bf16[256,512]{1,0:T(8,128)(2,1)S(1)}, ...), condition=%wide.region_17.18_spmd, body=%wide.region_16.17_spmd.sunk | while | flops 134479872 | bytes 2753675 | solution.py:114
  155.8 3.4 %fusion.28 = bf16[256,1024]{1,0:T(8,128)(2,1)} fusion(f32[256,1024]{1,0:T(8,128)S(1)} %get-tuple-element.162, f32[]{:T(128)S(6)} %div.51, f32[]{:T(128)S(6)} %mul.148, f32[]{:T(128)} %fusion.35, f32[]{:T(128)S(6)} %div.49, f32[]{:T(128)S(6)} %mul.140, f32[]{:T(128)S(6)} %mul.137, f32[256,1024]{1,0:T(8,128)S(1)} %gather_fusion, ...), kind=kLoop, calls=%fused_computation.46 | loop fusion | flops 4980736 | bytes 4195612 | tf_op jit(solution)/shard_map/convert_element_type | solution.py:107
  159.9 12.3 %all-gather.12.cloned.1.call-done = bf16[512,1024]{1,0:T(8,128)(2,1)} async-done(((bf16[256,1024]{1,0:T(8,128)(2,1)}), bf16[512,1024]{1,0:T(8,128)(2,1)}) %all-gather.12.cloned.1.call-update) | async-done | bytes 1048592 | tf_op jit(solution)/shard_map/all_gather | solution.py:107
  172.4 5.1 %while.53 = (s32[]{:T(128)}, f32[256,1024]{1,0:T(8,128)S(1)}, s32[]{:T(128)}, bf16[256,512]{1,0:T(8,128)(2,1)S(1)}, bf16[512,1024]{1,0:T(8,128)(2,1)}, /*index=5*/s32[]{:T(128)}, s32[]{:T(128)}, s32[]{:T(128)}, s32[]{:T(128)}) while((s32[]{:T(128)}, f32[256,1024]{1,0:T(8,128)S(1)}, s32[]{:T(128)}, bf16[256,512]{1,0:T(8,128)(2,1)S(1)}, ...), condition=%wide.region_19.20_spmd, body=%wide.region_18.19_spmd.sunk | while | flops 134479872 | bytes 2753675 | solution.py:114
  177.5 3.8 %add_convert_fusion = bf16[256,1024]{1,0:T(8,128)(2,1)} fusion(f32[256,1024]{1,0:T(8,128)S(1)} %get-tuple-element.163, f32[256,1024]{1,0:T(8,128)S(1)} %get-tuple-element.162, f32[]{:T(128)S(6)} %div.53, f32[]{:T(128)S(6)} %mul.155, f32[]{:T(128)S(6)} %div.51, f32[]{:T(128)S(6)} %mul.148, f32[]{:T(128)} %fusion.35, f32[]{:T(128)S(6)} %div.49, f32[]{:T(128)S(6)} %mul.140, ...), kind=kLoop, calls=%fused_computation.40 | loop fusion | flops 7340032 | bytes 5244196 | tf_op jit(solution)/shard_map/convert_element_type | solution.py:120
  181.3 2.9 subtract_convert_fusion
  184.2 10.2 %all-gather.14.cloned.1.call-done = bf16[512,1024]{1,0:T(8,128)(2,1)} async-done(((bf16[256,1024]{1,0:T(8,128)(2,1)}), bf16[512,1024]{1,0:T(8,128)(2,1)}) %all-gather.14.cloned.1.call-update) | async-done | bytes 1048592 | tf_op jit(solution)/shard_map/all_gather | solution.py:120
  194.3 2.5 broadcast_in_dim.60
  196.9 21.8 %while.54 = (s32[]{:T(128)}, f32[1024,1024]{1,0:T(8,128)}, s32[]{:T(128)}, bf16[512,1024]{1,0:T(8,128)(2,1)}, f32[2]{0:T(128)S(1)}, /*index=5*/bf16[512,1024]{1,...) while((s32[]{:T(128)}, f32[1024,1024]{1,0:T(8,128)}, ...), condition=%wide.region_22.23_spmd, body=%wide.region_20.22_spmd.sunk | while | flops 1075576832 | bytes 11536043 | solution.py:136
  199.9 6.2 %convolution_add_fusion.11 = f32[1024,1024]{1,0:T(8,128)} fusion(f32[1024,1024]{1,0:T(8,128)} %get-tuple-element.608, bf16[1024,1024]{1,0:T(8,128)(2,1)S(1)} %get-tuple-element.624, bf16[512,1024]{1,0:T(8,128)(2,1)S(1)} %get-tuple-element.623, s32[]{:T(128)S(6)} %select_n.155, f32[]{:T(128)} %fusion.66, bf16[512,1024]{1,0:T(8,128)(2,1)} %get-tuple-element.621), kind=kOutput, calls=%fused_computation.23.clone.1 | convolution fusion | flops 1075576832 | bytes 11535872 | tf_op jit(solution)/shard_map/while/body/dot_general | solution.py:132
  210.1 6.2 %convolution_add_fusion.11 = f32[1024,1024]{1,0:T(8,128)} fusion(f32[1024,1024]{1,0:T(8,128)} %get-tuple-element.608, bf16[1024,1024]{1,0:T(8,128)(2,1)S(1)} %get-tuple-element.624, bf16[512,1024]{1,0:T(8,128)(2,1)S(1)} %get-tuple-element.623, s32[]{:T(128)S(6)} %select_n.155, f32[]{:T(128)} %fusion.66, bf16[512,1024]{1,0:T(8,128)(2,1)} %get-tuple-element.621), kind=kOutput, calls=%fused_computation.23.clone.1 | convolution fusion | flops 1075576832 | bytes 11535872 | tf_op jit(solution)/shard_map/while/body/dot_general | solution.py:132
  218.7 2.5 convert_bitcast_fusion.1
  221.8 3.0 %reduce.4 = bf16[1024,1024]{1,0:T(8,128)(2,1)} reduce(bf16[1024,1,1,1024]{3,0,2,1:T(8,128)(2,1)S(1)} %convert_bitcast_fusion.1, bf16[]{:T(256)} %broadcast.165), dimensions={1,2}, to_apply=%copy.38.reduce_sub_computation | reduce | bytes 4194306 | tf_op jit(solution)/shard_map/convert_element_type | solution.py:140
  224.8 4.5 %reshape.108 = bf16[64,2,8192]{2,1,0:T(2,128)(2,1)} reshape(bf16[1024,1024]{1,0:T(8,128)(2,1)} %reduce.4) | data formatting | bytes 4194304
  229.2 40.8 %all_to_all.24 = bf16[64,2,8192]{2,1,0:T(2,128)(2,1)S(1)} all-to-all(bf16[64,2,8192]{2,1,0:T(2,128)(2,1)} %reshape.108), channel_id=1, replica_groups=mesh['member'=64,'region'=2] {'member'}, dimensions={0} | all-to-all | bytes 4194304 | tf_op jit(solution)/shard_map/all_to_all | solution.py:139
  270.0 6.7 %reshape.109 = bf16[1024,1,1,1024]{3,2,1,0:T(2,128)(2,1)} reshape(bf16[64,2,8192]{2,1,0:T(2,128)(2,1)S(1)} %all_to_all.24) | data formatting | bytes 4194304
  276.7 3.0 %copy.39 = bf16[1024,1,1,1024]{3,0,2,1:T(8,128)(2,1)S(1)} copy(bf16[1024,1,1,1024]{3,2,1,0:T(2,128)(2,1)} %reshape.109) | data formatting | bytes 4194304 | tf_op jit(solution)/shard_map/all_to_all | solution.py:139
  280.2 6.3 %copy.40 = f32[16,64,1,1024]{3,2,1,0:T(1,128)} copy(f32[16,64,1,1024]{3,0,1,2:T(8,128)S(1)} %convert_bitcast_fusion) | data formatting | bytes 8388608 | tf_op jit(solution)/shard_map/convert_element_type | solution.py:145
  (58 shorter events, 22.7 us)
Async XLA Ops:
  13.2 12.0 %copy-start.5 = (s32[1,1,256]{2,1,0:T(1,128)S(1)}, s32[1,1,256]{2,1,0:T(1,128)}, u32[]{:S(2)}) copy-start(s32[1,1,256]{2,1,0:T(1,128)} %param.17) | copy-start | bytes 3076
  13.2 66.6 %all-to-all-start = ((f32[16,64,1,1024]{3,0,2,1:T(8,128)}), f32[16,64,1,1024]{3,0,2,1:T(8,128)}, u32[]{:S(2)}, u32[]{:S(2)}) async-start(f32[16,64,1,1024]{3,0,2,1:T(8,128)} %copy.33), calls=%async_computation | async-start | bytes 8388608 | tf_op jit(solution)/shard_map/all_to_all | solution.py:60
  25.1 78.9 %all-gather.6.cloned.1.call-start = ((), (), s32[]{:S(2)}) async-start(), calls=%async_computation.2 | async-start | bytes 1572864 | tf_op jit(solution)/shard_map/all_gather | solution.py:88
  87.6 6.3 %copy-start.4 = (s32[1,2]{1,0:T(1,128)S(1)}, s32[1,2]{1,0:T(1,128)}, u32[]{:S(2)}) copy-start(s32[1,2]{1,0:T(1,128)} %param.21) | copy-start | bytes 28
  87.6 7.7 %copy-start.6 = (s32[1,2]{1,0:T(1,128)S(1)}, s32[1,2]{1,0:T(1,128)}, u32[]{:S(2)}) copy-start(s32[1,2]{1,0:T(1,128)} %param.20) | copy-start | bytes 28
  91.4 64.4 %copy-start = (f32[256,1024]{1,0:T(8,128)}, f32[256,1024]{1,0:T(8,128)S(1)}, u32[]{:S(2)}) copy-start(f32[256,1024]{1,0:T(8,128)S(1)} %gather_fusion) | copy-start | bytes 3145732
  93.7 22.9 %copy-start.1 = (bf16[1,1,256,1024]{3,2,1,0:T(8,128)(2,1)S(1)}, bf16[1,1,256,1024]{3,2,1,0:T(8,128)(2,1)}, u32[]{:S(2)}) copy-start(bf16[1,1,256,1024]{3,2,1,0:T(8,128)(2,1)} %param.19) | copy-start | bytes 1572868
  93.7 22.9 %copy-start.3 = (f32[1,1,256]{2,1,0:T(1,128)S(1)}, f32[1,1,256]{2,1,0:T(1,128)}, u32[]{:S(2)}) copy-start(f32[1,1,256]{2,1,0:T(1,128)} %param.18) | copy-start | bytes 3076
  93.8 37.0 %all-gather.8.cloned.1.call-start = ((), (), s32[]{:S(2)}) async-start(), calls=%async_computation.3 | async-start | bytes 1572864 | tf_op jit(solution)/shard_map/all_gather | solution.py:107
  117.8 33.0 %all-gather.10.cloned.1.call-start = ((), (), s32[]{:S(2)}) async-start(), calls=%async_computation.4 | async-start | bytes 1572864 | tf_op jit(solution)/shard_map/all_gather | solution.py:107
  137.8 34.5 %all-gather.12.cloned.1.call-start = ((), (), s32[]{:S(2)}) async-start(), calls=%async_computation.5 | async-start | bytes 1572864 | tf_op jit(solution)/shard_map/all_gather | solution.py:107
  159.2 35.1 %all-gather.14.cloned.1.call-start = ((), (), s32[]{:S(2)}) async-start(), calls=%async_computation.6 | async-start | bytes 1572864 | tf_op jit(solution)/shard_map/all_gather | solution.py:120
  181.3 15.6 %copy-start.2 = (bf16[512,1024]{1,0:T(8,128)(2,1)S(1)}, bf16[512,1024]{1,0:T(8,128)(2,1)}, u32[]{:S(2)}) copy-start(bf16[512,1024]{1,0:T(8,128)(2,1)} %get-tuple-element.639) | copy-start | bytes 3145732
Sparse Core Ops, SparseCore 0:
  93.9 10.0 all-gather.5
  117.9 12.8 all-gather.7
  137.9 12.8 all-gather.9
  159.4 12.8 all-gather.11
  181.4 12.8 all-gather.13
where the time goes:
time: 294 us; the launch traced here: 293 us
  waiting for transfers between devices  108 us (37%)
  blocking collectives  43.9 us (15%)
  local copies, waits for them, and re-layouts  41.3 us (14%)
  other arithmetic  29.7 us (10%)
  matrix products  24.9 us (8%)
  between operations  17.9 us (6%)
  loops' own time  15.7 us (5%)
  starting transfers between devices  12.1 us (4%)
    all_to_all x1, waiting for transfers between devices, shards(): lax.all_to_all(prior_samples, 'member', split_axis=1, concat_axis=0, tile...  54.6 us
    all_to_all x1, blocking collectives, shards(): lax.all_to_all(increment.reshape(sample_fields, 1, 1, cell_count).astype(...  40.8 us
    all_gather x3, waiting for transfers between devices, apply_rows(): lax.all_gather(direction.astype(jnp.bfloat16), 'region', axis=0, tiled=True)  36.7 us
    unnamed x17, local copies, waits for them, and re-layouts  17.9 us
    dot_general x2, matrix products, add_gain(): lax.dot_general(solved_rows, gain, (((0,), (1,)), ((), ())), preferred_el...  12.4 us
    all_to_all x1, starting transfers between devices, shards(): lax.all_to_all(prior_samples, 'member', split_axis=1, concat_axis=0, tile...  11.9 us
    all_gather x1, waiting for transfers between devices, shards(): lax.all_gather(local_solution.astype(jnp.bfloat16), 'region', axis=0, til...  10.2 us
    dot_general x6, matrix products, add_tile(): jnp.dot(weights_tile, source_rows, preferred_element_type=jnp.float32)  8.25 us
  transfers between devices with their start and end apart: 6, of which 6 were waited for; matrix products, arithmetic and copies ran while one was open for 2% of the time, Pallas kernels for 0%

commit v1 on v0

v1 whole, which is shorter than its diff:
```python
import jax
import jax.numpy as jnp
from jax import lax
from jax.experimental import pallas as pl
from jax.experimental.pallas import tpu as pltpu
from jax.sharding import PartitionSpec as P

ITERS = 4
TAPER_BASE = 0.7
LANES = 128
BANDS_PER_STEP = 8
VMEM = 56 * 1024 * 1024

f32 = jnp.float32
bf16 = jnp.bfloat16


def split3(value):
    high = value.astype(bf16)
    rest = value - high.astype(f32)
    middle = rest.astype(bf16)
    low = (rest - middle.astype(f32)).astype(bf16)
    return high, middle, low


def pack_members(x_ref, out_ref):
    members, bands, chunks, lanes = x_ref.shape
    cells = chunks * lanes
    flat = x_ref.reshape(members * bands * chunks, lanes)

    for band in range(bands):
        mean = jnp.sum(x_ref[:, band], axis=0) * (1.0 / members)
        high = mean.astype(bf16)
        low = (mean - high.astype(f32)).astype(bf16)
        held = high.astype(f32) + low.astype(f32)
        out_ref[band, :, cells : cells + lanes] = jnp.concatenate([high, low], axis=0)
        for chunk in range(chunks):
            rows = flat[pl.ds(band * chunks + chunk, members, stride=bands * chunks), :]
            out_ref[band, :, chunk * lanes : (chunk + 1) * lanes] = (
                rows - held[chunk : chunk + 1, :]
            ).astype(bf16)


def unpack_members(x_ref, out_ref):
    bands, members, cells = x_ref.shape
    chunks = cells // LANES
    flat = out_ref.reshape(members * bands * chunks, LANES)
    for band in range(bands):
        for chunk in range(chunks):
            flat[pl.ds(band * chunks + chunk, members, stride=bands * chunks), :] = x_ref[
                band, :, chunk * LANES : (chunk + 1) * LANES
            ].astype(f32)


def observe(x_ref, points_ref, readings_ref, anomaly_ref, seen_ref, means, spread, hot):
    sources, members, width = x_ref.shape
    cells = anomaly_ref.shape[1]
    total_members = anomaly_ref.shape[0]
    chunks = cells // LANES
    obs = points_ref.shape[1]

    for source in range(sources):
        tail = x_ref[source, :, cells:width].astype(f32)
        means[source] = tail[:chunks] + tail[chunks:]
    average = jnp.sum(means[...], axis=0) * (1.0 / sources)

    points = jnp.transpose(jnp.broadcast_to(points_ref[...], (LANES, obs)))
    lane = lax.broadcasted_iota(jnp.int32, (obs, LANES), 1)
    picked = jnp.zeros((obs, LANES), f32)
    for chunk in range(chunks):
        here = points == lane + chunk * LANES
        hot[:, chunk * LANES : (chunk + 1) * LANES] = jnp.where(here, 1.0, 0.0).astype(bf16)
        picked = picked + jnp.where(here, average[chunk : chunk + 1, :], 0.0)
    readings = jnp.transpose(jnp.broadcast_to(readings_ref[...], (LANES, obs)))
    base = readings - jnp.sum(picked, axis=1, keepdims=True)
    high, middle, low = split3(base)
    seen_ref[:, total_members : total_members + LANES] = jnp.where(
        lane == 0, high.astype(f32), jnp.where(lane == 1, middle.astype(f32), low.astype(f32))
    ).astype(bf16)

    spread[...] = means[...] - average[None]

    per_block = 16

    @pl.loop(0, sources // per_block)
    def _(block):
        for inner in range(per_block):
            source = block * per_block + inner
            rows = pl.ds(pl.multiple_of(source * members, members), members)
            shift = spread[source]
            for chunk in range(chunks):
                columns = slice(chunk * LANES, (chunk + 1) * LANES)
                anomaly_ref[rows, columns] = (
                    x_ref[source, :, columns].astype(f32) + shift[chunk : chunk + 1, :]
                ).astype(bf16)
        size = per_block * members
        span = pl.ds(pl.multiple_of(block * size, size), size)
        seen_ref[:, span] = lax.dot_general(
            hot[...],
            anomaly_ref[span, :],
            (((1,), (1,)), ((), ())),
            preferred_element_type=f32,
        ).astype(bf16)


def analyse(
    kinds_ref,
    groups_ref,
    anomaly_ref,
    own_ref,
    other_ref,
    own_noise_ref,
    other_noise_ref,
    out_ref,
    seen,
    covariance,
    gain,
    solved,
    residual,
    direction,
    tally,
):
    total_members, cells = anomaly_ref.shape
    tile = own_ref.shape[0]
    rows = 2 * tile
    region = lax.axis_index("region")
    own_kind = kinds_ref[0, region]
    other_kind = kinds_ref[0, 1 - region]
    one = jnp.int32(1)
    own_variance = 0.5 * lax.shift_left(one, own_kind).astype(f32)
    other_variance = 0.5 * lax.shift_left(one, other_kind).astype(f32)
    cross_weight = jnp.where(groups_ref[0, 0] == groups_ref[0, 1], f32(TAPER_BASE), f32(0.0))
    count = total_members - 1

    seen[:tile, :] = own_ref[:, :total_members]
    seen[tile:, :] = other_ref[:, :total_members]
    in_own = lax.broadcasted_iota(jnp.int32, (rows, 1), 0) < tile
    variance = jnp.where(in_own, own_variance, other_variance)
    weight_rows = jnp.where(in_own, f32(1.0), cross_weight)

    largest = f32(0.0)
    for half in range(2):
        block = seen[half * tile : (half + 1) * tile, :]
        product = lax.dot_general(
            seen[...], block, (((1,), (1,)), ((), ())), preferred_element_type=f32
        )
        weight = jnp.where(in_own == (half == 0), f32(1.0), cross_weight)
        covariance[:, half * tile : (half + 1) * tile] = (weight * product / count).astype(bf16)
    bound = variance + jnp.sum(jnp.abs(covariance[...].astype(f32)), axis=1, keepdims=True)
    largest = jnp.max(bound)
    lowest = jnp.minimum(own_variance, other_variance)
    highest = lowest + largest
    center = 0.5 * (highest + lowest)
    radius = 0.5 * (highest - lowest)
    sigma = center / radius
    rho = 1.0 / sigma

    own_base = jnp.sum(own_ref[:, total_members:].astype(f32)[:, :3], axis=1, keepdims=True)
    other_base = jnp.sum(other_ref[:, total_members:].astype(f32)[:, :3], axis=1, keepdims=True)
    own_scale = jnp.sqrt(jnp.full((1, 1), own_variance, f32))
    other_scale = jnp.sqrt(jnp.full((1, 1), other_variance, f32))
    width = residual.shape[1]

    steps = []
    for _ in range(ITERS - 1):
        rho_next = 1.0 / (2.0 * sigma - rho)
        steps.append((rho_next * rho, 2.0 * rho_next / radius))
        rho = rho_next

    @pl.loop(0, total_members // width)
    def _(block):
        span = pl.ds(pl.multiple_of(block * width, width), width)
        residual[:tile, :] = (
            own_base + own_scale * own_noise_ref[:, span].astype(f32) - own_ref[:, span].astype(f32)
        )
        residual[tile:, :] = (
            other_base
            + other_scale * other_noise_ref[:, span].astype(f32)
            - other_ref[:, span].astype(f32)
        )
        first = residual[...] / center
        direction[...] = first
        tally[...] = first
        for index, (keep, add) in enumerate(steps):
            now = direction[...]
            applied = variance * now + jnp.dot(
                covariance[...], now.astype(bf16), preferred_element_type=f32
            )
            left = residual[...] - applied
            later = keep * now + add * left
            if index < len(steps) - 1:
                residual[...] = left
                direction[...] = later
                tally[...] = tally[...] + later
            else:
                solved[:, span] = (tally[...] + later).astype(bf16)

    step = 256

    @pl.loop(0, cells // step)
    def _(block):
        span = pl.ds(pl.multiple_of(block * step, step), step)
        cross = jnp.dot(seen[...], anomaly_ref[:, span], preferred_element_type=f32)
        gain[:, span] = (weight_rows * cross / count).astype(bf16)

    @pl.loop(0, total_members // step)
    def _(block):
        span = pl.ds(pl.multiple_of(block * step, step), step)
        out_ref[span, :] = lax.dot_general(
            solved[:, span], gain[...], (((0,), (0,)), ((), ())), preferred_element_type=f32
        ).astype(bf16)


def whole(shape):
    return pl.BlockSpec(shape, lambda *_: (0,) * len(shape), memory_space=pltpu.VMEM)


def shards(
    prior_samples, measured_point, measured_reading, measurement_noise, noise_kind, taper_set
):
    members, bands, _, cells = prior_samples.shape
    tile = measured_point.shape[2]
    total = measurement_noise.shape[3]
    chunks = cells // LANES
    width = cells + LANES
    swap = [(0, 1), (1, 0)]

    own_noise = measurement_noise.reshape(tile, total)
    other_noise = lax.ppermute(own_noise, "region", swap)

    packed = pl.pallas_call(
        pack_members,
        grid=(bands // BANDS_PER_STEP,),
        in_specs=[
            pl.BlockSpec((members, BANDS_PER_STEP, chunks, LANES), lambda i: (0, i, 0, 0))
        ],
        out_specs=pl.BlockSpec((BANDS_PER_STEP, members, width), lambda i: (i, 0, 0)),
        out_shape=jax.ShapeDtypeStruct((bands, members, width), bf16),
        name="pack_members",
    )(prior_samples.reshape(members, bands, chunks, LANES))

    arrived = lax.all_to_all(packed, "member", split_axis=0, concat_axis=0, tiled=True)

    anomaly, seen = pl.pallas_call(
        observe,
        in_specs=[pl.BlockSpec(memory_space=pltpu.VMEM)] * 3,
        out_specs=[pl.BlockSpec(memory_space=pltpu.VMEM)] * 2,
        out_shape=[
            jax.ShapeDtypeStruct((total, cells), bf16),
            jax.ShapeDtypeStruct((tile, total + LANES), bf16),
        ],
        scratch_shapes=[
            pltpu.VMEM((bands, chunks, LANES), f32),
            pltpu.VMEM((bands, chunks, LANES), f32),
            pltpu.VMEM((tile, cells), bf16),
        ],
        compiler_params=pltpu.CompilerParams(vmem_limit_bytes=VMEM),
        name="observe",
    )(arrived, measured_point.reshape(1, tile), measured_reading.reshape(1, tile))

    other_seen = lax.ppermute(seen, "region", swap)

    increment = pl.pallas_call(
        analyse,
        in_specs=[pl.BlockSpec(memory_space=pltpu.SMEM)] * 2
        + [pl.BlockSpec(memory_space=pltpu.VMEM)] * 5,
        out_specs=pl.BlockSpec(memory_space=pltpu.VMEM),
        out_shape=jax.ShapeDtypeStruct((total, cells), bf16),
        scratch_shapes=[
            pltpu.VMEM((2 * tile, total), bf16),
            pltpu.VMEM((2 * tile, 2 * tile), bf16),
            pltpu.VMEM((2 * tile, cells), bf16),
            pltpu.VMEM((2 * tile, total), bf16),
            pltpu.VMEM((2 * tile, 256), f32),
            pltpu.VMEM((2 * tile, 256), f32),
            pltpu.VMEM((2 * tile, 256), f32),
        ],
        compiler_params=pltpu.CompilerParams(vmem_limit_bytes=VMEM),
        name="analyse",
    )(noise_kind, taper_set, anomaly, seen, other_seen, own_noise, other_noise)

    returned = lax.all_to_all(
        increment.reshape(bands, members, cells), "member", split_axis=0, concat_axis=0, tiled=True
    )

    unpacked = pl.pallas_call(
        unpack_members,
        grid=(bands // BANDS_PER_STEP,),
        in_specs=[pl.BlockSpec((BANDS_PER_STEP, members, cells), lambda i: (i, 0, 0))],
        out_specs=pl.BlockSpec((members, BANDS_PER_STEP, chunks, LANES), lambda i: (0, i, 0, 0)),
        out_shape=jax.ShapeDtypeStruct((members, bands, chunks, LANES), f32),
        name="unpack_members",
    )(returned)
    return unpacked.reshape(members, bands, 1, cells)


def solution(mesh):
    return jax.shard_map(
        shards,
        mesh=mesh,
        in_specs=(
            P("member", None, "region", None),
            P("member", "region", None),
            P("member", "region", None),
            P("member", "region", None, None),
            P("member", None),
            P("member", None),
        ),
        out_specs=P("member", None, "region", None),
        check_vma=False,
    )
```

time: 294 us -> 118 us (0.40)
  waiting for transfers between devices: 108 us -> 2.24 us
  local copies, waits for them, and re-layouts: 41.3 us -> 1 us
  blocking collectives: 43.9 us -> 80.8 us
  Pallas kernels: 0 us -> 32.6 us
  other arithmetic: 29.7 us -> 0 us
  matrix products: 24.9 us -> 0 us
  between operations: 17.9 us -> 0.01 us
  loops' own time: 15.7 us -> 0 us
  starting transfers between devices: 12.1 us -> 0.51 us
    all_to_all x1 -> x0, waiting for transfers between devices: 54.6 us -> none  [shards(): lax.all_to_all(prior_samples, 'member', split_axis=1, concat_axis=0, tile...]
    all_gather x5 -> x0, waiting for transfers between devices: 52.9 us -> none  [the longest x3 36.7 us: apply_rows(): lax.all_gather(direction.astype(jnp.bfloat16), 'region', axis=0, tiled=True)]
    all_to_all x1 -> x2, blocking collectives: 40.8 us -> 80.8 us  [the longest x1 44.7 us: shards(): lax.all_to_all(packed, 'member', split_axis=0, concat_axis=0, tiled=True)]
    pallas_call x0 -> x4, Pallas kernels: none -> 32.6 us  [the longest x1 12.7 us: shards(): pl.pallas_call(analyse, in_specs=[pl.BlockSpec(memory_space=pltpu.SMEM)]...]
    dot_general x10 -> x0, matrix products: 24.9 us -> none  [the longest x2 12.4 us: add_gain(): lax.dot_general(solved_rows, gain, (((0,), (1,)), ((), ())), preferred_el...]
    convert_element_type x9 -> x0, other arithmetic: 20 us -> none  [the longest x3 6.43 us: apply_rows(): direction.astype(jnp.bfloat16)]
    unnamed x17 -> x6, local copies, waits for them, and re-layouts: 17.9 us -> 1 us
    another operation x5 -> x0, loops' own time: 15.7 us -> none  [the longest x1 7.03 us: shards(): lax.fori_loop(first_block, last_block, add_gain, jnp.zeros((sample_fields...]
  transfers between devices with their start and end apart: 6 -> 2, of which waited for: 6 -> 1; matrix products, arithmetic and copies ran while one was open for 2% -> 0% of each run, Pallas kernels for 0% -> 0%
where the time goes in v1:
time: 118 us; the launch traced here: 117 us
  blocking collectives  80.8 us (68%)
  Pallas kernels  32.6 us (28%)
  waiting for transfers between devices  2.24 us (2%)
    all_to_all x1, blocking collectives, shards(): lax.all_to_all(packed, 'member', split_axis=0, concat_axis=0, tiled=True)  44.7 us
    all_to_all x1, blocking collectives, shards(): lax.all_to_all(increment.reshape(bands, members, cells), 'member', split_...  36.2 us
    pallas_call x1, Pallas kernels, shards(): pl.pallas_call(analyse, in_specs=[pl.BlockSpec(memory_space=pltpu.SMEM)]...  12.7 us
    pallas_call x1, Pallas kernels, shards(): pl.pallas_call(unpack_members, grid=(bands // BANDS_PER_STEP,), in_specs=...  7.56 us
    pallas_call x1, Pallas kernels, shards(): pl.pallas_call(pack_members, grid=(bands // BANDS_PER_STEP,), in_specs=[p...  7.32 us
    pallas_call x1, Pallas kernels, shards(): pl.pallas_call(observe, in_specs=[pl.BlockSpec(memory_space=pltpu.VMEM)]...  5.07 us
  transfers between devices with their start and end apart: 2, of which 1 were waited for; matrix products, arithmetic and copies ran while one was open for 0% of the time, Pallas kernels for 0%

profile of v1, /device:TPU:0, one launch (start us, length us, event | category | flops | bytes accessed | tf_op | source)
XLA Modules:
  0.0 117.2 jit_solution(13539129104633475452)
XLA Ops:
  0.0 7.3 %pack_members.1 = bf16[64,16,1152]{2,1,0:T(8,128)(2,1)} custom-call(f32[16,64,8,128]{3,2,1,0:T(8,128)} %bitcast.7), custom_call_target="tpu_custom_call" | custom-call | tf_op jit(solution)/shard_map/pack_members/pallas_call | solution.py:231
  7.3 44.7 %all_to_all.10.x_ref = bf16[64,16,1152]{2,1,0:T(8,128)(2,1)} all-to-all(bf16[64,16,1152]{2,1,0:T(8,128)(2,1)} %pack_members.1), channel_id=1, replica_groups=mesh['member'=64,'region'=2] {'member'}, dimensions={0} | all-to-all | bytes 4718592 | tf_op jit(solution)/shard_map/all_to_all | solution.py:242
  52.0 0.0 copy-start.1
  52.0 5.1 %observe.1 = (bf16[1024,1024]{1,0:T(8,128)(2,1)}, bf16[256,1152]{1,0:T(8,128)(2,1)}) custom-call(bf16[64,16,1152]{2,1,0:T(8,128)(2,1)} %all_to_all.10.x_ref, s32[1,256]{1,0:T(1,128)} %bitcast.10, f32[1,256]{1,0:T(1,128)} %bitcast.11), custom_call_target="tpu_custom_call" | custom-call | tf_op jit(solution)/shard_map/observe/pallas_call | solution.py:244
  57.1 0.0 collective-permute-start
  57.1 0.0 copy-done.1
  57.1 0.5 collective-permute-start.1
  57.6 2.2 %collective-permute-done.1.other_noise_ref = bf16[256,1024]{1,0:T(8,128)(2,1)S(1)} collective-permute-done((bf16[256,1024]{1,0:T(8,128)(2,1)S(1)}, bf16[256,1024]{1,0:T(8,128)(2,1)S(1)}, u32[]{:S(2)}, u32[]{:S(2)}) %collective-permute-start.1) | collective-permute-done | bytes 524320 | tf_op jit(solution)/shard_map/ppermute | solution.py:229
  59.8 0.0 copy-start.2
  59.8 0.0 collective-permute-done.other_ref
  59.8 0.0 copy-start
  59.8 0.8 copy-done.2
  60.6 0.2 copy-done
  60.8 12.7 %analyse.1 = bf16[1024,1024]{1,0:T(8,128)(2,1)} custom-call(s32[1,2]{1,0:T(1,128)} %kinds_ref.1, s32[1,2]{1,0:T(1,128)} %groups_ref.1, bf16[1024,1024]{1,0:T(8,128)(2,1)} %get-tuple-element.7.anomaly_ref, bf16[256,1152]{1,0:T(8,128)(2,1)} %get-tuple-element.8.own_ref, bf16[256,1152]{1,0:T(8,128)(2,1)} %copy-done, bf16[256,1024]{1,0:T(8,128)(2,1)} %bitcast.8, ...), custom_call_target="tpu_custom_call" | custom-call | tf_op jit(solution)/shard_map/analyse/pallas_call | solution.py:263
  73.5 36.2 %all_to_all.11.x_ref = bf16[64,16,1024]{2,1,0:T(8,128)(2,1)} all-to-all(bf16[64,16,1024]{2,1,0:T(8,128)(2,1)} %bitcast.6), channel_id=1, replica_groups=mesh['member'=64,'region'=2] {'member'}, dimensions={0} | all-to-all | bytes 4194304 | tf_op jit(solution)/shard_map/all_to_all | solution.py:282
  109.6 7.6 %unpack_members.1 = f32[16,64,8,128]{3,2,1,0:T(8,128)} custom-call(bf16[64,16,1024]{2,1,0:T(8,128)(2,1)} %all_to_all.11.x_ref), custom_call_target="tpu_custom_call" | custom-call | tf_op jit(solution)/shard_map/unpack_members/pallas_call | solution.py:286
Async XLA Ops:
  52.0 5.1 %copy-start.1 = (bf16[1,1,256,1024]{3,2,1,0:T(8,128)(2,1)S(1)}, bf16[1,1,256,1024]{3,2,1,0:T(8,128)(2,1)}, u32[]{:S(2)}) copy-start(bf16[1,1,256,1024]{3,2,1,0:T(8,128)(2,1)} %param.9) | copy-start | bytes 1572868
  57.1 2.8 %collective-permute-start = (bf16[256,1152]{1,0:T(8,128)(2,1)}, bf16[256,1152]{1,0:T(8,128)(2,1)S(1)}, u32[]{:S(2)}, u32[]{:S(2)}) collective-permute-start(bf16[256,1152]{1,0:T(8,128)(2,1)} %get-tuple-element.8.own_ref), channel_id=1, source_target_pairs={{0,1},{1,0},{2,3},{3,2},{4,5},{5,4},{6,7},{7,6},{8,9},{9,8},{10,11... | collective-permute-start | bytes 1769480 | tf_op jit(solution)/shard_map/ppermute | solution.py:261
  57.1 2.7 %collective-permute-start.1 = (bf16[256,1024]{1,0:T(8,128)(2,1)S(1)}, bf16[256,1024]{1,0:T(8,128)(2,1)S(1)}, u32[]{:S(2)}, u32[]{:S(2)}) collective-permute-start(bf16[256,1024]{1,0:T(8,128)(2,1)S(1)} %bitcast.9), channel_id=1, source_target_pairs={{0,1},{1,0},{2,3},{3,2},{4,5},{5,4},{6,7},{7,6},{8,9},{9,8},{10,11... | collective-permute-start | bytes 1572872 | tf_op jit(solution)/shard_map/ppermute | solution.py:229
  59.8 0.8 copy-start.2
  59.8 1.0 copy-start

commit v2 on v1

--- a/solution.py
+++ b/solution.py
@@ -9,7 +9,7 @@
 TAPER_BASE = 0.7
 LANES = 128
 BANDS_PER_STEP = 8
-VMEM = 56 * 1024 * 1024
+MIB = 1024 * 1024
 
 f32 = jnp.float32
 bf16 = jnp.bfloat16
@@ -23,33 +23,56 @@
     return high, middle, low
 
 
+def row_order(rows, members, chunks):
+    to = lax.broadcasted_iota(jnp.int32, (rows, rows), 0)
+    source = lax.broadcasted_iota(jnp.int32, (rows, rows), 1)
+    wanted = lax.rem(to, members) * chunks + lax.div(to, members)
+    return jnp.where(source == wanted, 1.0, 0.0).astype(bf16)
+
+
 def pack_members(x_ref, out_ref):
     members, bands, chunks, lanes = x_ref.shape
     cells = chunks * lanes
-    flat = x_ref.reshape(members * bands * chunks, lanes)
-
-    for band in range(bands):
-        mean = jnp.sum(x_ref[:, band], axis=0) * (1.0 / members)
-        high = mean.astype(bf16)
-        low = (mean - high.astype(f32)).astype(bf16)
-        held = high.astype(f32) + low.astype(f32)
-        out_ref[band, :, cells : cells + lanes] = jnp.concatenate([high, low], axis=0)
-        for chunk in range(chunks):
-            rows = flat[pl.ds(band * chunks + chunk, members, stride=bands * chunks), :]
-            out_ref[band, :, chunk * lanes : (chunk + 1) * lanes] = (
-                rows - held[chunk : chunk + 1, :]
-            ).astype(bf16)
+    rows = members * chunks
+    order = row_order(rows, members, chunks)
+    for pair in range(bands // 2):
+        parts = []
+        for band in (2 * pair, 2 * pair + 1):
+            values = x_ref[:, band]
+            mean = jnp.sum(values, axis=0) * (1.0 / members)
+            high = mean.astype(bf16)
+            low = (mean - high.astype(f32)).astype(bf16)
+            held = high.astype(f32) + low.astype(f32)
+            out_ref[band, :, cells : cells + lanes] = jnp.concatenate([high, low], axis=0)
+            parts.append((values - held[None]).reshape(rows, lanes).astype(bf16))
+        moved = jnp.dot(
+            order, jnp.concatenate(parts, axis=1), preferred_element_type=f32
+        ).astype(bf16)
+        for index in range(2):
+            for chunk in range(chunks):
+                out_ref[2 * pair + index, :, chunk * lanes : (chunk + 1) * lanes] = moved[
+                    chunk * members : (chunk + 1) * members, index * lanes : (index + 1) * lanes
+                ]
 
 
 def unpack_members(x_ref, out_ref):
     bands, members, cells = x_ref.shape
     chunks = cells // LANES
-    flat = out_ref.reshape(members * bands * chunks, LANES)
-    for band in range(bands):
-        for chunk in range(chunks):
-            flat[pl.ds(band * chunks + chunk, members, stride=bands * chunks), :] = x_ref[
-                band, :, chunk * LANES : (chunk + 1) * LANES
-            ].astype(f32)
+    rows = members * chunks
+    order = row_order(rows, chunks, members)
+    for pair in range(bands // 2):
+        parts = []
+        for band in (2 * pair, 2 * pair + 1):
+            parts.append(
+                jnp.concatenate(
+                    [x_ref[band, :, c * LANES : (c + 1) * LANES] for c in range(chunks)], axis=0
+                )
+            )
+        moved = jnp.dot(order, jnp.concatenate(parts, axis=1), preferred_element_type=f32)
+        for index in range(2):
+            out_ref[:, 2 * pair + index] = moved[
+                :, index * LANES : (index + 1) * LANES
+            ].reshape(members, chunks, LANES)
 
 
 def observe(x_ref, points_ref, readings_ref, anomaly_ref, seen_ref, means, spread, hot):
@@ -116,9 +139,9 @@
     covariance,
     gain,
     solved,
-    residual,
-    direction,
-    tally,
+    zero,
+    one_step,
+    two_steps,
 ):
     total_members, cells = anomaly_ref.shape
     tile = own_ref.shape[0]
@@ -138,14 +161,13 @@
     variance = jnp.where(in_own, own_variance, other_variance)
     weight_rows = jnp.where(in_own, f32(1.0), cross_weight)
 
-    largest = f32(0.0)
     for half in range(2):
         block = seen[half * tile : (half + 1) * tile, :]
         product = lax.dot_general(
             seen[...], block, (((1,), (1,)), ((), ())), preferred_element_type=f32
         )
         weight = jnp.where(in_own == (half == 0), f32(1.0), cross_weight)
-        covariance[:, half * tile : (half + 1) * tile] = (weight * product / count).astype(bf16)
+        covariance[:, half * tile : (half + 1) * tile] = (product * (weight / count)).astype(bf16)
     bound = variance + jnp.sum(jnp.abs(covariance[...].astype(f32)), axis=1, keepdims=True)
     largest = jnp.max(bound)
     lowest = jnp.minimum(own_variance, other_variance)
@@ -159,41 +181,50 @@
     other_base = jnp.sum(other_ref[:, total_members:].astype(f32)[:, :3], axis=1, keepdims=True)
     own_scale = jnp.sqrt(jnp.full((1, 1), own_variance, f32))
     other_scale = jnp.sqrt(jnp.full((1, 1), other_variance, f32))
-    width = residual.shape[1]
+    width = zero.shape[1]
 
     steps = []
+    reach_before, keep_before = 1.0 / center, f32(0.0)
     for _ in range(ITERS - 1):
         rho_next = 1.0 / (2.0 * sigma - rho)
-        steps.append((rho_next * rho, 2.0 * rho_next / radius))
-        rho = rho_next
+        keep = rho_next * rho
+        reach = 2.0 * rho_next / radius
+        ratio = reach / reach_before
+        steps.append((keep + ratio - reach * variance, ratio * keep_before, reach))
+        rho, reach_before, keep_before = rho_next, reach, keep
+    inverse = 1.0 / center
 
     @pl.loop(0, total_members // width)
     def _(block):
         span = pl.ds(pl.multiple_of(block * width, width), width)
-        residual[:tile, :] = (
+        zero[:tile, :] = inverse * (
             own_base + own_scale * own_noise_ref[:, span].astype(f32) - own_ref[:, span].astype(f32)
         )
-        residual[tile:, :] = (
+        zero[tile:, :] = inverse * (
             other_base
             + other_scale * other_noise_ref[:, span].astype(f32)
             - other_ref[:, span].astype(f32)
         )
-        first = residual[...] / center
-        direction[...] = first
-        tally[...] = first
-        for index, (keep, add) in enumerate(steps):
-            now = direction[...]
-            applied = variance * now + jnp.dot(
-                covariance[...], now.astype(bf16), preferred_element_type=f32
-            )
-            left = residual[...] - applied
-            later = keep * now + add * left
-            if index < len(steps) - 1:
-                residual[...] = left
-                direction[...] = later
-                tally[...] = tally[...] + later
-            else:
-                solved[:, span] = (tally[...] + later).astype(bf16)
+        ahead, _, reach = steps[0]
+        now = zero[...]
+        one_step[...] = ahead * now - reach * jnp.dot(
+            covariance[...], now.astype(bf16), preferred_element_type=f32
+        )
+        ahead, back, reach = steps[1]
+        now = one_step[...]
+        two_steps[...] = (
+            ahead * now
+            - back * zero[...]
+            - reach * jnp.dot(covariance[...], now.astype(bf16), preferred_element_type=f32)
+        )
+        ahead, back, reach = steps[2]
+        now = two_steps[...]
+        solved[:, span] = (
+            (1.0 + ahead) * now
+            + (1.0 - back) * one_step[...]
+            + zero[...]
+            - reach * jnp.dot(covariance[...], now.astype(bf16), preferred_element_type=f32)
+        ).astype(bf16)
 
     step = 256
 
@@ -201,7 +232,7 @@
     def _(block):
         span = pl.ds(pl.multiple_of(block * step, step), step)
         cross = jnp.dot(seen[...], anomaly_ref[:, span], preferred_element_type=f32)
-        gain[:, span] = (weight_rows * cross / count).astype(bf16)
+        gain[:, span] = (cross * (weight_rows / count)).astype(bf16)
 
     @pl.loop(0, total_members // step)
     def _(block):
@@ -236,9 +267,14 @@
         ],
         out_specs=pl.BlockSpec((BANDS_PER_STEP, members, width), lambda i: (i, 0, 0)),
         out_shape=jax.ShapeDtypeStruct((bands, members, width), bf16),
+        cost_estimate=pl.CostEstimate(
+            flops=4 * members * bands * cells, bytes_accessed=7 * members * bands * cells, transcendentals=0
+        ),
+        compiler_params=pltpu.CompilerParams(vmem_limit_bytes=12 * MIB),
         name="pack_members",
     )(prior_samples.reshape(members, bands, chunks, LANES))
 
+    packed, other_noise = lax.optimization_barrier((packed, other_noise))
     arrived = lax.all_to_all(packed, "member", split_axis=0, concat_axis=0, tiled=True)
 
     anomaly, seen = pl.pallas_call(
@@ -254,7 +290,7 @@
             pltpu.VMEM((bands, chunks, LANES), f32),
             pltpu.VMEM((tile, cells), bf16),
         ],
-        compiler_params=pltpu.CompilerParams(vmem_limit_bytes=VMEM),
+        compiler_params=pltpu.CompilerParams(vmem_limit_bytes=12 * MIB),
         name="observe",
     )(arrived, measured_point.reshape(1, tile), measured_reading.reshape(1, tile))
 
@@ -275,7 +311,7 @@
             pltpu.VMEM((2 * tile, 256), f32),
             pltpu.VMEM((2 * tile, 256), f32),
         ],
-        compiler_params=pltpu.CompilerParams(vmem_limit_bytes=VMEM),
+        compiler_params=pltpu.CompilerParams(vmem_limit_bytes=20 * MIB),
         name="analyse",
     )(noise_kind, taper_set, anomaly, seen, other_seen, own_noise, other_noise)
 
@@ -289,6 +325,7 @@
         in_specs=[pl.BlockSpec((BANDS_PER_STEP, members, cells), lambda i: (i, 0, 0))],
         out_specs=pl.BlockSpec((members, BANDS_PER_STEP, chunks, LANES), lambda i: (0, i, 0, 0)),
         out_shape=jax.ShapeDtypeStruct((members, bands, chunks, LANES), f32),
+        compiler_params=pltpu.CompilerParams(vmem_limit_bytes=12 * MIB),
         name="unpack_members",
     )(returned)
     return unpacked.reshape(members, bands, 1, cells)

time: 118 us -> 103 us (0.87)
  Pallas kernels: 32.6 us -> 18.5 us
  local copies, waits for them, and re-layouts: 1 us -> 2.21 us
    pallas_call x1, Pallas kernels: 7.32 us -> 2.42 us  [shards(): pl.pallas_call(pack_members, grid=(bands // BANDS_PER_STEP,), in_specs=[p...]
    pallas_call x1, Pallas kernels: 7.56 us -> 4.3 us  [shards(): pl.pallas_call(unpack_members, grid=(bands // BANDS_PER_STEP,), in_specs=...]
    pallas_call x1, Pallas kernels: 12.7 us -> 9.6 us  [shards(): pl.pallas_call(analyse, in_specs=[pl.BlockSpec(memory_space=pltpu.SMEM)]...]
    pallas_call x1, Pallas kernels: 5.07 us -> 2.16 us  [shards(): pl.pallas_call(observe, in_specs=[pl.BlockSpec(memory_space=pltpu.VMEM)]...]
    ppermute x1, waiting for transfers between devices: 2.24 us -> 0.01 us  [shards(): other_noise = lax.ppermute(own_noise, 'region', swap)]
    ppermute x1, waiting for transfers between devices: 0.01 us -> 1.99 us  [shards(): other_seen = lax.ppermute(seen, 'region', swap)]
    unnamed x6 -> x12, local copies, waits for them, and re-layouts: 1 us -> 2.21 us
  transfers between devices with their start and end apart: 2 -> 2, of which waited for: 1 -> 1; matrix products, arithmetic and copies ran while one was open for 0% -> 0% of each run, Pallas kernels for 0% -> 2%
where the time goes in v2:
time: 103 us
  blocking collectives  80.4 us (78%)
  Pallas kernels  18.5 us (18%)
  local copies, waits for them, and re-layouts  2.21 us (2%)
  waiting for transfers between devices  1.99 us (2%)
    all_to_all x1, blocking collectives, shards(): lax.all_to_all(packed, 'member', split_axis=0, concat_axis=0, tiled=True)  45 us
    all_to_all x1, blocking collectives, shards(): lax.all_to_all(increment.reshape(bands, members, cells), 'member', split_...  35.4 us
    pallas_call x1, Pallas kernels, shards(): pl.pallas_call(analyse, in_specs=[pl.BlockSpec(memory_space=pltpu.SMEM)]...  9.6 us
    pallas_call x1, Pallas kernels, shards(): pl.pallas_call(unpack_members, grid=(bands // BANDS_PER_STEP,), in_specs=...  4.3 us
    pallas_call x1, Pallas kernels, shards(): pl.pallas_call(pack_members, grid=(bands // BANDS_PER_STEP,), in_specs=[p...  2.42 us
    unnamed x12, local copies, waits for them, and re-layouts  2.21 us
    pallas_call x1, Pallas kernels, shards(): pl.pallas_call(observe, in_specs=[pl.BlockSpec(memory_space=pltpu.VMEM)]...  2.16 us
  transfers between devices with their start and end apart: 2, of which 1 were waited for; matrix products, arithmetic and copies ran while one was open for 0% of the time, Pallas kernels for 2%

profile of v2, /device:TPU:0, one launch (start us, length us, event | category | flops | bytes accessed | tf_op | source)
XLA Modules:
  0.0 103.3 jit_solution(17090978787463451651)
XLA Ops:
  0.0 0.0 collective-permute-start
  0.0 0.0 copy-start
  0.0 2.2 %copy-done = f32[16,64,1,1024]{3,2,1,0:T(1,128)S(1)} copy-done((f32[16,64,1,1024]{3,2,1,0:T(1,128)S(1)}, f32[16,64,1,1024]{3,2,1,0:T(1,128)}, u32[]{:S(2)}) %copy-start) | copy-done | bytes 4194328
  2.2 2.4 %pack_members.1 = bf16[64,16,1152]{2,1,0:T(8,128)(2,1)S(1)} custom-call(f32[16,64,8,128]{3,2,1,0:T(8,128)S(1)} %bitcast.7), custom_call_target="tpu_custom_call" | custom-call | flops 4194304 | bytes 7340032 | tf_op jit(solution)/shard_map/pack_members/pallas_call | solution.py:262
  4.6 0.0 copy-start.2
  4.6 0.0 copy-start.3
  4.6 0.0 collective-permute-done.other_noise_ref
  4.7 45.0 %all_to_all.10.x_ref = bf16[64,16,1152]{2,1,0:T(8,128)(2,1)S(1)} all-to-all(bf16[64,16,1152]{2,1,0:T(8,128)(2,1)S(1)} %pack_members.1), channel_id=1, replica_groups=mesh['member'=64,'region'=2] {'member'}, dimensions={0} | all-to-all | bytes 4718592 | tf_op jit(solution)/shard_map/all_to_all | solution.py:278
  49.7 0.0 copy-start.1
  49.7 0.0 copy-start.4
  49.7 0.0 copy-start.5
  49.7 0.0 copy-done.2
  49.7 0.0 copy-done.3
  49.7 2.2 %observe.1 = (bf16[1024,1024]{1,0:T(8,128)(2,1)S(1)}, bf16[256,1152]{1,0:T(8,128)(2,1)S(1)}) custom-call(bf16[64,16,1152]{2,1,0:T(8,128)(2,1)S(1)} %all_to_all.10.x_ref, s32[1,256]{1,0:T(1,128)S(1)} %bitcast.10, f32[1,256]{1,0:T(1,128)S(1)} %bitcast.11), custom_call_target="tpu_custom_call" | custom-call | tf_op jit(solution)/shard_map/observe/pallas_call | solution.py:280
  51.9 0.1 collective-permute-start.1
  52.0 2.0 %collective-permute-done.1.other_ref = bf16[256,1152]{1,0:T(8,128)(2,1)S(1)} collective-permute-done((bf16[256,1152]{1,0:T(8,128)(2,1)S(1)}, bf16[256,1152]{1,0:T(8,128)(2,1)S(1)}, u32[]{:S(2)}, u32[]{:S(2)}) %collective-permute-start.1) | collective-permute-done | bytes 589856 | tf_op jit(solution)/shard_map/ppermute | solution.py:297
  54.0 0.0 copy-done.1
  54.0 0.0 copy-done.4
  54.0 0.0 copy-done.5
  54.0 9.6 %analyse.1 = bf16[1024,1024]{1,0:T(8,128)(2,1)S(1)} custom-call(s32[1,2]{1,0:T(1,128)S(1)} %copy-done.4, s32[1,2]{1,0:T(1,128)S(1)} %copy-done.5, bf16[1024,1024]{1,0:T(8,128)(2,1)S(1)} %get-tuple-element.10.anomaly_ref, bf16[256,1152]{1,0:T(8,128)(2,1)S(1)} %get-tuple-element.11.own_ref, bf16[256,1152]{1,0:T(8,128)(2,1)S(1)} %collective-permute-done.1.other_ref, ...), custom_call_target="tpu_custom_call" | custom-call | tf_op jit(solution)/shard_map/analyse/pallas_call | solution.py:299
  63.6 35.4 %all_to_all.11.x_ref = bf16[64,16,1024]{2,1,0:T(8,128)(2,1)S(1)} all-to-all(bf16[64,16,1024]{2,1,0:T(8,128)(2,1)S(1)} %bitcast.6), channel_id=1, replica_groups=mesh['member'=64,'region'=2] {'member'}, dimensions={0} | all-to-all | bytes 4194304 | tf_op jit(solution)/shard_map/all_to_all | solution.py:318
  99.0 4.3 %unpack_members.1 = f32[16,64,8,128]{3,2,1,0:T(8,128)} custom-call(bf16[64,16,1024]{2,1,0:T(8,128)(2,1)S(1)} %all_to_all.11.x_ref), custom_call_target="tpu_custom_call" | custom-call | tf_op jit(solution)/shard_map/unpack_members/pallas_call | solution.py:322
Async XLA Ops:
  0.0 4.6 %collective-permute-start = (bf16[256,1024]{1,0:T(8,128)(2,1)}, bf16[256,1024]{1,0:T(8,128)(2,1)S(1)}, u32[]{:S(2)}, u32[]{:S(2)}) collective-permute-start(bf16[256,1024]{1,0:T(8,128)(2,1)} %bitcast.8), channel_id=1, source_target_pairs={{0,1},{1,0},{2,3},{3,2},{4,5},{5,4},{6,7},{7,6},{8,9},{9,8},{10,11... | collective-permute-start | bytes 1572872 | tf_op jit(solution)/shard_map/ppermute | solution.py:260
  0.0 2.2 %copy-start = (f32[16,64,1,1024]{3,2,1,0:T(1,128)S(1)}, f32[16,64,1,1024]{3,2,1,0:T(1,128)}, u32[]{:S(2)}) copy-start(f32[16,64,1,1024]{3,2,1,0:T(1,128)} %param.6) | copy-start | bytes 12582916
  4.6 45.1 %copy-start.2 = (s32[1,1,256]{2,1,0:T(1,128)S(1)}, s32[1,1,256]{2,1,0:T(1,128)}, u32[]{:S(2)}) copy-start(s32[1,1,256]{2,1,0:T(1,128)} %param.7) | copy-start | bytes 3076
  4.6 45.1 %copy-start.3 = (f32[1,1,256]{2,1,0:T(1,128)S(1)}, f32[1,1,256]{2,1,0:T(1,128)}, u32[]{:S(2)}) copy-start(f32[1,1,256]{2,1,0:T(1,128)} %param.8) | copy-start | bytes 3076
  49.7 4.3 %copy-start.1 = (bf16[1,1,256,1024]{3,2,1,0:T(8,128)(2,1)S(1)}, bf16[1,1,256,1024]{3,2,1,0:T(8,128)(2,1)}, u32[]{:S(2)}) copy-start(bf16[1,1,256,1024]{3,2,1,0:T(8,128)(2,1)} %param.9) | copy-start | bytes 1572868
  49.7 4.3 %copy-start.4 = (s32[1,2]{1,0:T(1,128)S(1)}, s32[1,2]{1,0:T(1,128)}, u32[]{:S(2)}) copy-start(s32[1,2]{1,0:T(1,128)} %kinds_ref.1) | copy-start | bytes 28
  49.7 4.3 %copy-start.5 = (s32[1,2]{1,0:T(1,128)S(1)}, s32[1,2]{1,0:T(1,128)}, u32[]{:S(2)}) copy-start(s32[1,2]{1,0:T(1,128)} %groups_ref.1) | copy-start | bytes 28
  51.9 2.1 %collective-permute-start.1 = (bf16[256,1152]{1,0:T(8,128)(2,1)S(1)}, bf16[256,1152]{1,0:T(8,128)(2,1)S(1)}, u32[]{:S(2)}, u32[]{:S(2)}) collective-permute-start(bf16[256,1152]{1,0:T(8,128)(2,1)S(1)} %get-tuple-element.11.own_ref), channel_id=1, source_target_pairs={{0,1},{1,0},{2,3},{3,2},{4,5},{5,4},{6,7},{7,6},{8,9},{9,8},{10,11... | collective-permute-start | bytes 1769480 | tf_op jit(solution)/shard_map/ppermute | solution.py:297

commit v3 on v2

--- a/solution.py
+++ b/solution.py
@@ -8,7 +8,8 @@
 ITERS = 4
 TAPER_BASE = 0.7
 LANES = 128
-BANDS_PER_STEP = 8
+GROUPS = 8
+COLUMNS = 512
 MIB = 1024 * 1024
 
 f32 = jnp.float32
@@ -30,49 +31,72 @@
     return jnp.where(source == wanted, 1.0, 0.0).astype(bf16)
 
 
-def pack_members(x_ref, out_ref):
+def pack_members(x_ref, out_ref, held, arrived):
     members, bands, chunks, lanes = x_ref.shape
     cells = chunks * lanes
     rows = members * chunks
+    groups = arrived.shape[0]
+    per_group = bands // groups
+
+    def fetch(group):
+        span = pl.ds(group * per_group, per_group)
+        return pltpu.make_async_copy(x_ref.at[:, span], held.at[:, span], arrived.at[group])
+
+    for group in range(groups):
+        fetch(group).start()
     order = row_order(rows, members, chunks)
-    for pair in range(bands // 2):
-        parts = []
-        for band in (2 * pair, 2 * pair + 1):
-            values = x_ref[:, band]
-            mean = jnp.sum(values, axis=0) * (1.0 / members)
-            high = mean.astype(bf16)
-            low = (mean - high.astype(f32)).astype(bf16)
-            held = high.astype(f32) + low.astype(f32)
-            out_ref[band, :, cells : cells + lanes] = jnp.concatenate([high, low], axis=0)
-            parts.append((values - held[None]).reshape(rows, lanes).astype(bf16))
-        moved = jnp.dot(
-            order, jnp.concatenate(parts, axis=1), preferred_element_type=f32
-        ).astype(bf16)
-        for index in range(2):
-            for chunk in range(chunks):
-                out_ref[2 * pair + index, :, chunk * lanes : (chunk + 1) * lanes] = moved[
-                    chunk * members : (chunk + 1) * members, index * lanes : (index + 1) * lanes
-                ]
-
-
-def unpack_members(x_ref, out_ref):
+    for group in range(groups):
+        fetch(group).wait()
+        for pair in range(group * per_group // 2, (group + 1) * per_group // 2):
+            parts = []
+            for band in (2 * pair, 2 * pair + 1):
+                values = held[:, band]
+                mean = jnp.sum(values, axis=0) * (1.0 / members)
+                high = mean.astype(bf16)
+                low = (mean - high.astype(f32)).astype(bf16)
+                middle = high.astype(f32) + low.astype(f32)
+                out_ref[band, :, cells : cells + lanes] = jnp.concatenate([high, low], axis=0)
+                parts.append((values - middle[None]).reshape(rows, lanes).astype(bf16))
+            moved = jnp.dot(
+                order, jnp.concatenate(parts, axis=1), preferred_element_type=f32
+            ).astype(bf16)
+            for index in range(2):
+                for chunk in range(chunks):
+                    out_ref[2 * pair + index, :, chunk * lanes : (chunk + 1) * lanes] = moved[
+                        chunk * members : (chunk + 1) * members,
+                        index * lanes : (index + 1) * lanes,
+                    ]
+
+
+def unpack_members(x_ref, out_ref, held, sent):
     bands, members, cells = x_ref.shape
     chunks = cells // LANES
     rows = members * chunks
+    groups = sent.shape[0]
+    per_group = bands // groups
     order = row_order(rows, chunks, members)
-    for pair in range(bands // 2):
-        parts = []
-        for band in (2 * pair, 2 * pair + 1):
-            parts.append(
-                jnp.concatenate(
-                    [x_ref[band, :, c * LANES : (c + 1) * LANES] for c in range(chunks)], axis=0
+
+    def put(group):
+        span = pl.ds(group * per_group, per_group)
+        return pltpu.make_async_copy(held.at[:, span], out_ref.at[:, span], sent.at[group])
+
+    for group in range(groups):
+        for pair in range(group * per_group // 2, (group + 1) * per_group // 2):
+            parts = []
+            for band in (2 * pair, 2 * pair + 1):
+                parts.append(
+                    jnp.concatenate(
+                        [x_ref[band, :, c * LANES : (c + 1) * LANES] for c in range(chunks)], axis=0
+                    )
                 )
-            )
-        moved = jnp.dot(order, jnp.concatenate(parts, axis=1), preferred_element_type=f32)
-        for index in range(2):
-            out_ref[:, 2 * pair + index] = moved[
-                :, index * LANES : (index + 1) * LANES
-            ].reshape(members, chunks, LANES)
+            moved = jnp.dot(order, jnp.concatenate(parts, axis=1), preferred_element_type=f32)
+            for index in range(2):
+                held[:, 2 * pair + index] = moved[
+                    :, index * LANES : (index + 1) * LANES
+                ].reshape(members, chunks, LANES)
+        put(group).start()
+    for group in range(groups):
+        put(group).wait()
 
 
 def observe(x_ref, points_ref, readings_ref, anomaly_ref, seen_ref, means, spread, hot):
@@ -161,13 +185,13 @@
     variance = jnp.where(in_own, own_variance, other_variance)
     weight_rows = jnp.where(in_own, f32(1.0), cross_weight)
 
+    product = lax.dot_general(
+        seen[...], seen[...], (((1,), (1,)), ((), ())), preferred_element_type=f32
+    )
     for half in range(2):
-        block = seen[half * tile : (half + 1) * tile, :]
-        product = lax.dot_general(
-            seen[...], block, (((1,), (1,)), ((), ())), preferred_element_type=f32
-        )
+        columns = slice(half * tile, (half + 1) * tile)
         weight = jnp.where(in_own == (half == 0), f32(1.0), cross_weight)
-        covariance[:, half * tile : (half + 1) * tile] = (product * (weight / count)).astype(bf16)
+        covariance[:, columns] = (product[:, columns] * (weight / count)).astype(bf16)
     bound = variance + jnp.sum(jnp.abs(covariance[...].astype(f32)), axis=1, keepdims=True)
     largest = jnp.max(bound)
     lowest = jnp.minimum(own_variance, other_variance)
@@ -181,7 +205,7 @@
     other_base = jnp.sum(other_ref[:, total_members:].astype(f32)[:, :3], axis=1, keepdims=True)
     own_scale = jnp.sqrt(jnp.full((1, 1), own_variance, f32))
     other_scale = jnp.sqrt(jnp.full((1, 1), other_variance, f32))
-    width = zero.shape[1]
+    width = COLUMNS
 
     steps = []
     reach_before, keep_before = 1.0 / center, f32(0.0)
@@ -194,56 +218,44 @@
         rho, reach_before, keep_before = rho_next, reach, keep
     inverse = 1.0 / center
 
-    @pl.loop(0, total_members // width)
-    def _(block):
-        span = pl.ds(pl.multiple_of(block * width, width), width)
-        zero[:tile, :] = inverse * (
+    spans = [slice(start, start + width) for start in range(0, total_members, width)]
+    for span in spans:
+        zero[:tile, span] = inverse * (
             own_base + own_scale * own_noise_ref[:, span].astype(f32) - own_ref[:, span].astype(f32)
         )
-        zero[tile:, :] = inverse * (
+        zero[tile:, span] = inverse * (
             other_base
             + other_scale * other_noise_ref[:, span].astype(f32)
             - other_ref[:, span].astype(f32)
         )
+
+    def apply(held, span):
+        return jnp.dot(
+            covariance[...], held[:, span].astype(bf16), preferred_element_type=f32
+        )
+
+    for span in spans:
         ahead, _, reach = steps[0]
-        now = zero[...]
-        one_step[...] = ahead * now - reach * jnp.dot(
-            covariance[...], now.astype(bf16), preferred_element_type=f32
+        one_step[:, span] = ahead * zero[:, span] - reach * apply(zero, span)
+    for span in spans:
+        ahead, back, reach = steps[1]
+        two_steps[:, span] = (
+            ahead * one_step[:, span] - back * zero[:, span] - reach * apply(one_step, span)
         )
-        ahead, back, reach = steps[1]
-        now = one_step[...]
-        two_steps[...] = (
-            ahead * now
-            - back * zero[...]
-            - reach * jnp.dot(covariance[...], now.astype(bf16), preferred_element_type=f32)
-        )
+    for span in spans:
         ahead, back, reach = steps[2]
-        now = two_steps[...]
         solved[:, span] = (
-            (1.0 + ahead) * now
-            + (1.0 - back) * one_step[...]
-            + zero[...]
-            - reach * jnp.dot(covariance[...], now.astype(bf16), preferred_element_type=f32)
+            (1.0 + ahead) * two_steps[:, span]
+            + (1.0 - back) * one_step[:, span]
+            + zero[:, span]
+            - reach * apply(two_steps, span)
         ).astype(bf16)
 
-    step = 256
-
-    @pl.loop(0, cells // step)
-    def _(block):
-        span = pl.ds(pl.multiple_of(block * step, step), step)
-        cross = jnp.dot(seen[...], anomaly_ref[:, span], preferred_element_type=f32)
-        gain[:, span] = (cross * (weight_rows / count)).astype(bf16)
-
-    @pl.loop(0, total_members // step)
-    def _(block):
-        span = pl.ds(pl.multiple_of(block * step, step), step)
-        out_ref[span, :] = lax.dot_general(
-            solved[:, span], gain[...], (((0,), (0,)), ((), ())), preferred_element_type=f32
-        ).astype(bf16)
-
-
-def whole(shape):
-    return pl.BlockSpec(shape, lambda *_: (0,) * len(shape), memory_space=pltpu.VMEM)
+    cross = jnp.dot(seen[...], anomaly_ref[...], preferred_element_type=f32)
+    gain[...] = (cross * (weight_rows / count)).astype(bf16)
+    out_ref[...] = lax.dot_general(
+        solved[...], gain[...], (((0,), (0,)), ((), ())), preferred_element_type=f32
+    ).astype(bf16)
 
 
 def shards(
@@ -261,16 +273,17 @@
 
     packed = pl.pallas_call(
         pack_members,
-        grid=(bands // BANDS_PER_STEP,),
-        in_specs=[
-            pl.BlockSpec((members, BANDS_PER_STEP, chunks, LANES), lambda i: (0, i, 0, 0))
-        ],
-        out_specs=pl.BlockSpec((BANDS_PER_STEP, members, width), lambda i: (i, 0, 0)),
+        in_specs=[pl.BlockSpec(memory_space=pltpu.HBM)],
+        out_specs=pl.BlockSpec(memory_space=pltpu.VMEM),
         out_shape=jax.ShapeDtypeStruct((bands, members, width), bf16),
+        scratch_shapes=[
+            pltpu.VMEM((members, bands, chunks, LANES), f32),
+            pltpu.SemaphoreType.DMA((GROUPS,)),
+        ],
         cost_estimate=pl.CostEstimate(
             flops=4 * members * bands * cells, bytes_accessed=7 * members * bands * cells, transcendentals=0
         ),
-        compiler_params=pltpu.CompilerParams(vmem_limit_bytes=12 * MIB),
+        compiler_params=pltpu.CompilerParams(vmem_limit_bytes=57 * MIB),
         name="pack_members",
     )(prior_samples.reshape(members, bands, chunks, LANES))
 
@@ -307,11 +320,11 @@
             pltpu.VMEM((2 * tile, 2 * tile), bf16),
             pltpu.VMEM((2 * tile, cells), bf16),
             pltpu.VMEM((2 * tile, total), bf16),
-            pltpu.VMEM((2 * tile, 256), f32),
-            pltpu.VMEM((2 * tile, 256), f32),
-            pltpu.VMEM((2 * tile, 256), f32),
-        ],
-        compiler_params=pltpu.CompilerParams(vmem_limit_bytes=20 * MIB),
+            pltpu.VMEM((2 * tile, total), f32),
+            pltpu.VMEM((2 * tile, total), f32),
+            pltpu.VMEM((2 * tile, total), f32),
+        ],
+        compiler_params=pltpu.CompilerParams(vmem_limit_bytes=28 * MIB),
         name="analyse",
     )(noise_kind, taper_set, anomaly, seen, other_seen, own_noise, other_noise)
 
@@ -321,10 +334,13 @@
 
     unpacked = pl.pallas_call(
         unpack_members,
-        grid=(bands // BANDS_PER_STEP,),
-        in_specs=[pl.BlockSpec((BANDS_PER_STEP, members, cells), lambda i: (i, 0, 0))],
-        out_specs=pl.BlockSpec((members, BANDS_PER_STEP, chunks, LANES), lambda i: (0, i, 0, 0)),
+        in_specs=[pl.BlockSpec(memory_space=pltpu.VMEM)],
+        out_specs=pl.BlockSpec(memory_space=pltpu.HBM),
         out_shape=jax.ShapeDtypeStruct((members, bands, chunks, LANES), f32),
+        scratch_shapes=[
+            pltpu.VMEM((members, bands, chunks, LANES), f32),
+            pltpu.SemaphoreType.DMA((GROUPS,)),
+        ],
         compiler_params=pltpu.CompilerParams(vmem_limit_bytes=12 * MIB),
         name="unpack_members",
     )(returned)

time: 103 us -> 98.1 us (0.952)
  Pallas kernels: 18.5 us -> 15 us
  local copies, waits for them, and re-layouts: 2.21 us -> 0.02 us
    pallas_call x1, Pallas kernels: 9.6 us -> 6.08 us  [shards(): pl.pallas_call(analyse, in_specs=[pl.BlockSpec(memory_space=pltpu.SMEM)]...]
    unnamed x12 -> x10, local copies, waits for them, and re-layouts: 2.21 us -> 0.02 us
  transfers between devices with their start and end apart: 2 -> 2, of which waited for: 1 -> 1; matrix products, arithmetic and copies ran while one was open for 0% -> 0% of each run, Pallas kernels for 2% -> 5%
where the time goes in v3:
time: 98.1 us; the launch traced here: 97.9 us
  blocking collectives  80.6 us (82%)
  Pallas kernels  15 us (15%)
  waiting for transfers between devices  1.99 us (2%)
    all_to_all x1, blocking collectives, shards(): lax.all_to_all(packed, 'member', split_axis=0, concat_axis=0, tiled=True)  45.2 us
    all_to_all x1, blocking collectives, shards(): lax.all_to_all(increment.reshape(bands, members, cells), 'member', split_...  35.4 us
    pallas_call x1, Pallas kernels, shards(): pl.pallas_call(analyse, in_specs=[pl.BlockSpec(memory_space=pltpu.SMEM)]...  6.08 us
    pallas_call x1, Pallas kernels, shards(): pl.pallas_call(pack_members, in_specs=[pl.BlockSpec(memory_space=pltpu.HB...  4.52 us
    pallas_call x1, Pallas kernels, shards(): pl.pallas_call(unpack_members, in_specs=[pl.BlockSpec(memory_space=pltpu....  2.29 us
    pallas_call x1, Pallas kernels, shards(): pl.pallas_call(observe, in_specs=[pl.BlockSpec(memory_space=pltpu.VMEM)]...  2.15 us
    ppermute x1, waiting for transfers between devices, shards(): other_seen = lax.ppermute(seen, 'region', swap)  1.99 us
  transfers between devices with their start and end apart: 2, of which 1 were waited for; matrix products, arithmetic and copies ran while one was open for 0% of the time, Pallas kernels for 5%

profile of v3, /device:TPU:0, one launch (start us, length us, event | category | flops | bytes accessed | tf_op | source)
XLA Modules:
  0.0 97.9 jit_solution(2346189354943523051)
XLA Ops:
  0.0 0.0 collective-permute-start
  0.0 4.5 %pack_members.1 = bf16[64,16,1152]{2,1,0:T(8,128)(2,1)} custom-call(f32[16,64,8,128]{3,2,1,0:T(8,128)} %bitcast.11), custom_call_target="tpu_custom_call" | custom-call | flops 4194304 | bytes 7340032 | tf_op jit(solution)/shard_map/pack_members/pallas_call | solution.py:274
  4.5 0.0 copy-start.1
  4.5 0.0 copy-start.2
  4.6 0.0 collective-permute-done.other_noise_ref
  4.6 45.2 %all_to_all.10.x_ref = bf16[64,16,1152]{2,1,0:T(8,128)(2,1)S(1)} all-to-all(bf16[64,16,1152]{2,1,0:T(8,128)(2,1)} %pack_members.1), channel_id=1, replica_groups=mesh['member'=64,'region'=2] {'member'}, dimensions={0} | all-to-all | bytes 4718592 | tf_op jit(solution)/shard_map/all_to_all | solution.py:291
  49.8 0.0 copy-start
  49.8 0.0 copy-start.3
  49.8 0.0 copy-start.4
  49.8 0.0 copy-done.1
  49.8 0.0 copy-done.2
  49.8 2.2 %observe.1 = (bf16[1024,1024]{1,0:T(8,128)(2,1)S(1)}, bf16[256,1152]{1,0:T(8,128)(2,1)S(1)}) custom-call(bf16[64,16,1152]{2,1,0:T(8,128)(2,1)S(1)} %all_to_all.10.x_ref, s32[1,256]{1,0:T(1,128)S(1)} %bitcast.9, f32[1,256]{1,0:T(1,128)S(1)} %bitcast.10), custom_call_target="tpu_custom_call" | custom-call | tf_op jit(solution)/shard_map/observe/pallas_call | solution.py:293
  52.0 0.1 collective-permute-start.1
  52.1 2.0 %collective-permute-done.1.other_ref = bf16[256,1152]{1,0:T(8,128)(2,1)S(1)} collective-permute-done((bf16[256,1152]{1,0:T(8,128)(2,1)S(1)}, bf16[256,1152]{1,0:T(8,128)(2,1)S(1)}, u32[]{:S(2)}, u32[]{:S(2)}) %collective-permute-start.1) | collective-permute-done | bytes 589856 | tf_op jit(solution)/shard_map/ppermute | solution.py:310
  54.1 0.0 copy-done
  54.1 0.0 copy-done.3
  54.1 0.0 copy-done.4
  54.1 6.1 %analyse.1 = bf16[1024,1024]{1,0:T(8,128)(2,1)S(1)} custom-call(s32[1,2]{1,0:T(1,128)S(1)} %copy-done.3, s32[1,2]{1,0:T(1,128)S(1)} %copy-done.4, bf16[1024,1024]{1,0:T(8,128)(2,1)S(1)} %get-tuple-element.10.anomaly_ref, bf16[256,1152]{1,0:T(8,128)(2,1)S(1)} %get-tuple-element.11.own_ref, bf16[256,1152]{1,0:T(8,128)(2,1)S(1)} %collective-permute-done.1.other_ref, ...), custom_call_target="tpu_custom_call" | custom-call | tf_op jit(solution)/shard_map/analyse/pallas_call | solution.py:312
  60.2 35.4 %all_to_all.11.x_ref = bf16[64,16,1024]{2,1,0:T(8,128)(2,1)S(1)} all-to-all(bf16[64,16,1024]{2,1,0:T(8,128)(2,1)S(1)} %bitcast.6), channel_id=1, replica_groups=mesh['member'=64,'region'=2] {'member'}, dimensions={0} | all-to-all | bytes 4194304 | tf_op jit(solution)/shard_map/all_to_all | solution.py:331
  95.6 2.3 %unpack_members.1 = f32[16,64,8,128]{3,2,1,0:T(8,128)} custom-call(bf16[64,16,1024]{2,1,0:T(8,128)(2,1)S(1)} %all_to_all.11.x_ref), custom_call_target="tpu_custom_call" | custom-call | tf_op jit(solution)/shard_map/unpack_members/pallas_call | solution.py:335
Async XLA Ops:
  0.0 4.6 %collective-permute-start = (bf16[256,1024]{1,0:T(8,128)(2,1)}, bf16[256,1024]{1,0:T(8,128)(2,1)S(1)}, u32[]{:S(2)}, u32[]{:S(2)}) collective-permute-start(bf16[256,1024]{1,0:T(8,128)(2,1)} %bitcast.7), channel_id=1, source_target_pairs={{0,1},{1,0},{2,3},{3,2},{4,5},{5,4},{6,7},{7,6},{8,9},{9,8},{10,11... | collective-permute-start | bytes 1572872 | tf_op jit(solution)/shard_map/ppermute | solution.py:272
  4.5 45.3 %copy-start.1 = (s32[1,1,256]{2,1,0:T(1,128)S(1)}, s32[1,1,256]{2,1,0:T(1,128)}, u32[]{:S(2)}) copy-start(s32[1,1,256]{2,1,0:T(1,128)} %param.7) | copy-start | bytes 3076
  4.5 45.3 %copy-start.2 = (f32[1,1,256]{2,1,0:T(1,128)S(1)}, f32[1,1,256]{2,1,0:T(1,128)}, u32[]{:S(2)}) copy-start(f32[1,1,256]{2,1,0:T(1,128)} %param.8) | copy-start | bytes 3076
  49.8 4.3 %copy-start = (bf16[1,1,256,1024]{3,2,1,0:T(8,128)(2,1)S(1)}, bf16[1,1,256,1024]{3,2,1,0:T(8,128)(2,1)}, u32[]{:S(2)}) copy-start(bf16[1,1,256,1024]{3,2,1,0:T(8,128)(2,1)} %param.9) | copy-start | bytes 1572868
  49.8 4.3 %copy-start.3 = (s32[1,2]{1,0:T(1,128)S(1)}, s32[1,2]{1,0:T(1,128)}, u32[]{:S(2)}) copy-start(s32[1,2]{1,0:T(1,128)} %kinds_ref.1) | copy-start | bytes 28
  49.8 4.3 %copy-start.4 = (s32[1,2]{1,0:T(1,128)S(1)}, s32[1,2]{1,0:T(1,128)}, u32[]{:S(2)}) copy-start(s32[1,2]{1,0:T(1,128)} %groups_ref.1) | copy-start | bytes 28
  52.0 2.1 %collective-permute-start.1 = (bf16[256,1152]{1,0:T(8,128)(2,1)S(1)}, bf16[256,1152]{1,0:T(8,128)(2,1)S(1)}, u32[]{:S(2)}, u32[]{:S(2)}) collective-permute-start(bf16[256,1152]{1,0:T(8,128)(2,1)S(1)} %get-tuple-element.11.own_ref), channel_id=1, source_target_pairs={{0,1},{1,0},{2,3},{3,2},{4,5},{5,4},{6,7},{7,6},{8,9},{9,8},{10,11... | collective-permute-start | bytes 1769480 | tf_op jit(solution)/shard_map/ppermute | solution.py:310

commit v4 on v3

--- a/solution.py
+++ b/solution.py
@@ -12,8 +12,28 @@
 COLUMNS = 512
 MIB = 1024 * 1024
 
+STRIDE = 13
+
 f32 = jnp.float32
 bf16 = jnp.bfloat16
+
+
+def group_order(devices):
+    return [STRIDE * place % devices for place in range(devices)]
+
+
+def place_of(devices):
+    places = [0] * devices
+    for place, device in enumerate(group_order(devices)):
+        places[device] = place
+    return places
+
+
+def exchange(value):
+    order = group_order(value.shape[0])
+    return lax.all_to_all(
+        value, "member", split_axis=0, concat_axis=0, axis_index_groups=[order], tiled=True
+    )
 
 
 def split3(value):
@@ -45,6 +65,7 @@
     for group in range(groups):
         fetch(group).start()
     order = row_order(rows, members, chunks)
+    place = place_of(bands)
     for group in range(groups):
         fetch(group).wait()
         for pair in range(group * per_group // 2, (group + 1) * per_group // 2):
@@ -55,14 +76,14 @@
                 high = mean.astype(bf16)
                 low = (mean - high.astype(f32)).astype(bf16)
                 middle = high.astype(f32) + low.astype(f32)
-                out_ref[band, :, cells : cells + lanes] = jnp.concatenate([high, low], axis=0)
+                out_ref[place[band], :, cells : cells + lanes] = jnp.concatenate([high, low], axis=0)
                 parts.append((values - middle[None]).reshape(rows, lanes).astype(bf16))
             moved = jnp.dot(
                 order, jnp.concatenate(parts, axis=1), preferred_element_type=f32
             ).astype(bf16)
             for index in range(2):
                 for chunk in range(chunks):
-                    out_ref[2 * pair + index, :, chunk * lanes : (chunk + 1) * lanes] = moved[
+                    out_ref[place[2 * pair + index], :, chunk * lanes : (chunk + 1) * lanes] = moved[
                         chunk * members : (chunk + 1) * members,
                         index * lanes : (index + 1) * lanes,
                     ]
@@ -75,6 +96,7 @@
     groups = sent.shape[0]
     per_group = bands // groups
     order = row_order(rows, chunks, members)
+    place = place_of(bands)
 
     def put(group):
         span = pl.ds(group * per_group, per_group)
@@ -86,7 +108,10 @@
             for band in (2 * pair, 2 * pair + 1):
                 parts.append(
                     jnp.concatenate(
-                        [x_ref[band, :, c * LANES : (c + 1) * LANES] for c in range(chunks)], axis=0
+                        [
+                            x_ref[place[band], :, c * LANES : (c + 1) * LANES]
+                            for c in range(chunks)
+                        ], axis=0
                     )
                 )
             moved = jnp.dot(order, jnp.concatenate(parts, axis=1), preferred_element_type=f32)
@@ -106,8 +131,9 @@
     chunks = cells // LANES
     obs = points_ref.shape[1]
 
+    place = place_of(sources)
     for source in range(sources):
-        tail = x_ref[source, :, cells:width].astype(f32)
+        tail = x_ref[place[source], :, cells:width].astype(f32)
         means[source] = tail[:chunks] + tail[chunks:]
     average = jnp.sum(means[...], axis=0) * (1.0 / sources)
 
@@ -127,21 +153,16 @@
 
     spread[...] = means[...] - average[None]
 
-    per_block = 16
-
-    @pl.loop(0, sources // per_block)
-    def _(block):
-        for inner in range(per_block):
-            source = block * per_block + inner
-            rows = pl.ds(pl.multiple_of(source * members, members), members)
-            shift = spread[source]
-            for chunk in range(chunks):
-                columns = slice(chunk * LANES, (chunk + 1) * LANES)
-                anomaly_ref[rows, columns] = (
-                    x_ref[source, :, columns].astype(f32) + shift[chunk : chunk + 1, :]
-                ).astype(bf16)
-        size = per_block * members
-        span = pl.ds(pl.multiple_of(block * size, size), size)
+    for source in range(sources):
+        rows = slice(source * members, (source + 1) * members)
+        shift = spread[source]
+        for chunk in range(chunks):
+            columns = slice(chunk * LANES, (chunk + 1) * LANES)
+            anomaly_ref[rows, columns] = (
+                x_ref[place[source], :, columns].astype(f32) + shift[chunk : chunk + 1, :]
+            ).astype(bf16)
+    for start in range(0, total_members, COLUMNS):
+        span = slice(start, start + COLUMNS)
         seen_ref[:, span] = lax.dot_general(
             hot[...],
             anomaly_ref[span, :],
@@ -253,9 +274,12 @@
 
     cross = jnp.dot(seen[...], anomaly_ref[...], preferred_element_type=f32)
     gain[...] = (cross * (weight_rows / count)).astype(bf16)
-    out_ref[...] = lax.dot_general(
+    increment = lax.dot_general(
         solved[...], gain[...], (((0,), (0,)), ((), ())), preferred_element_type=f32
     ).astype(bf16)
+    devices, members, _ = out_ref.shape
+    for device, place in enumerate(place_of(devices)):
+        out_ref[place] = increment[device * members : (device + 1) * members]
 
 
 def shards(
@@ -283,12 +307,12 @@
         cost_estimate=pl.CostEstimate(
             flops=4 * members * bands * cells, bytes_accessed=7 * members * bands * cells, transcendentals=0
         ),
-        compiler_params=pltpu.CompilerParams(vmem_limit_bytes=57 * MIB),
+        compiler_params=pltpu.CompilerParams(vmem_limit_bytes=50 * MIB),
         name="pack_members",
     )(prior_samples.reshape(members, bands, chunks, LANES))
 
     packed, other_noise = lax.optimization_barrier((packed, other_noise))
-    arrived = lax.all_to_all(packed, "member", split_axis=0, concat_axis=0, tiled=True)
+    arrived = exchange(packed)
 
     anomaly, seen = pl.pallas_call(
         observe,
@@ -314,7 +338,7 @@
         in_specs=[pl.BlockSpec(memory_space=pltpu.SMEM)] * 2
         + [pl.BlockSpec(memory_space=pltpu.VMEM)] * 5,
         out_specs=pl.BlockSpec(memory_space=pltpu.VMEM),
-        out_shape=jax.ShapeDtypeStruct((total, cells), bf16),
+        out_shape=jax.ShapeDtypeStruct((bands, members, cells), bf16),
         scratch_shapes=[
             pltpu.VMEM((2 * tile, total), bf16),
             pltpu.VMEM((2 * tile, 2 * tile), bf16),
@@ -328,9 +352,7 @@
         name="analyse",
     )(noise_kind, taper_set, anomaly, seen, other_seen, own_noise, other_noise)
 
-    returned = lax.all_to_all(
-        increment.reshape(bands, members, cells), "member", split_axis=0, concat_axis=0, tiled=True
-    )
+    returned = exchange(increment)
 
     unpacked = pl.pallas_call(
         unpack_members,

time: 98.1 us -> 94.2 us (0.960)
  Pallas kernels: 15 us -> 12.9 us
  blocking collectives: 80.6 us -> 78.9 us
    all_to_all x2, blocking collectives: 80.6 us -> 78.9 us  [exchange(): lax.all_to_all(value, 'member', split_axis=0, concat_axis=0, axis_index_g...]
    pallas_call x1, Pallas kernels: 4.52 us -> 3.12 us  [shards(): pl.pallas_call(pack_members, in_specs=[pl.BlockSpec(memory_space=pltpu.HB...]
  transfers between devices with their start and end apart: 2 -> 2, of which waited for: 1 -> 1; matrix products, arithmetic and copies ran while one was open for 0% -> 0% of each run, Pallas kernels for 5% -> 3%
where the time goes in v4:
time: 94.2 us; the launch traced here: 94 us
  blocking collectives  78.9 us (84%)
  Pallas kernels  12.9 us (14%)
  waiting for transfers between devices  1.99 us (2%)
    all_to_all x2, blocking collectives, exchange(): lax.all_to_all(value, 'member', split_axis=0, concat_axis=0, axis_index_g...  78.9 us
    pallas_call x1, Pallas kernels, shards(): pl.pallas_call(analyse, in_specs=[pl.BlockSpec(memory_space=pltpu.SMEM)]...  6.09 us
    pallas_call x1, Pallas kernels, shards(): pl.pallas_call(pack_members, in_specs=[pl.BlockSpec(memory_space=pltpu.HB...  3.12 us
    pallas_call x1, Pallas kernels, shards(): pl.pallas_call(unpack_members, in_specs=[pl.BlockSpec(memory_space=pltpu....  2.29 us
    ppermute x1, waiting for transfers between devices, shards(): other_seen = lax.ppermute(seen, 'region', swap)  1.99 us
  transfers between devices with their start and end apart: 2, of which 1 were waited for; matrix products, arithmetic and copies ran while one was open for 0% of the time, Pallas kernels for 3%

profile of v4, /device:TPU:0, one launch (start us, length us, event | category | flops | bytes accessed | tf_op | source)
XLA Modules:
  0.0 94.0 jit_solution(8105208742137426288)
XLA Ops:
  0.0 0.0 collective-permute-start
  0.0 3.1 %pack_members.1 = bf16[64,16,1152]{2,1,0:T(8,128)(2,1)S(1)} custom-call(f32[16,64,8,128]{3,2,1,0:T(8,128)} %bitcast.9), custom_call_target="tpu_custom_call" | custom-call | flops 4194304 | bytes 7340032 | tf_op jit(solution)/shard_map/pack_members/pallas_call | solution.py:298
  3.1 0.0 copy-start.1
  3.1 0.0 copy-start.2
  3.2 0.0 collective-permute-done.other_noise_ref
  3.2 44.7 %all_to_all.10.x_ref = bf16[64,16,1152]{2,1,0:T(8,128)(2,1)S(1)} all-to-all(bf16[64,16,1152]{2,1,0:T(8,128)(2,1)S(1)} %pack_members.1), channel_id=1, replica_groups={{0,26,52,78,104,2,28,54,80,106,4,30,56,82,108,6,32,58,84,110,8,34,60,86..., dimensions={0} | all-to-all | bytes 4718592 | tf_op jit(solution)/shard_map/all_to_all | solution.py:34
  47.9 0.0 copy-start
  47.9 0.0 copy-start.3
  47.9 0.0 copy-start.4
  47.9 0.0 copy-done.1
  47.9 0.0 copy-done.2
  47.9 1.4 %observe.1 = (bf16[1024,1024]{1,0:T(8,128)(2,1)S(1)}, bf16[256,1152]{1,0:T(8,128)(2,1)S(1)}) custom-call(bf16[64,16,1152]{2,1,0:T(8,128)(2,1)S(1)} %all_to_all.10.x_ref, s32[1,256]{1,0:T(1,128)S(1)} %bitcast.7, f32[1,256]{1,0:T(1,128)S(1)} %bitcast.8), custom_call_target="tpu_custom_call" | custom-call | tf_op jit(solution)/shard_map/observe/pallas_call | solution.py:317
  49.3 0.1 collective-permute-start.1
  49.4 2.0 %collective-permute-done.1.other_ref = bf16[256,1152]{1,0:T(8,128)(2,1)S(1)} collective-permute-done((bf16[256,1152]{1,0:T(8,128)(2,1)S(1)}, bf16[256,1152]{1,0:T(8,128)(2,1)S(1)}, u32[]{:S(2)}, u32[]{:S(2)}) %collective-permute-start.1) | collective-permute-done | bytes 589856 | tf_op jit(solution)/shard_map/ppermute | solution.py:334
  51.4 0.0 copy-done
  51.4 0.0 copy-done.3
  51.4 0.0 copy-done.4
  51.4 6.1 %analyse.1 = bf16[64,16,1024]{2,1,0:T(8,128)(2,1)S(1)} custom-call(s32[1,2]{1,0:T(1,128)S(1)} %copy-done.3, s32[1,2]{1,0:T(1,128)S(1)} %copy-done.4, bf16[1024,1024]{1,0:T(8,128)(2,1)S(1)} %get-tuple-element.10.anomaly_ref, bf16[256,1152]{1,0:T(8,128)(2,1)S(1)} %get-tuple-element.11.own_ref, bf16[256,1152]{1,0:T(8,128)(2,1)S(1)} %collective-permute-done.1.other_ref, ...), custom_call_target="tpu_custom_call" | custom-call | tf_op jit(solution)/shard_map/analyse/pallas_call | solution.py:336
  57.5 34.2 %all_to_all.11.x_ref = bf16[64,16,1024]{2,1,0:T(8,128)(2,1)S(1)} all-to-all(bf16[64,16,1024]{2,1,0:T(8,128)(2,1)S(1)} %analyse.1), channel_id=1, replica_groups={{0,26,52,78,104,2,28,54,80,106,4,30,56,82,108,6,32,58,84,110,8,34,60,86..., dimensions={0} | all-to-all | bytes 4194304 | tf_op jit(solution)/shard_map/all_to_all | solution.py:34
  91.7 2.3 %unpack_members.1 = f32[16,64,8,128]{3,2,1,0:T(8,128)} custom-call(bf16[64,16,1024]{2,1,0:T(8,128)(2,1)S(1)} %all_to_all.11.x_ref), custom_call_target="tpu_custom_call" | custom-call | tf_op jit(solution)/shard_map/unpack_members/pallas_call | solution.py:357
Async XLA Ops:
  0.0 3.2 %collective-permute-start = (bf16[256,1024]{1,0:T(8,128)(2,1)}, bf16[256,1024]{1,0:T(8,128)(2,1)S(1)}, u32[]{:S(2)}, u32[]{:S(2)}) collective-permute-start(bf16[256,1024]{1,0:T(8,128)(2,1)} %bitcast.5), channel_id=1, source_target_pairs={{0,1},{1,0},{2,3},{3,2},{4,5},{5,4},{6,7},{7,6},{8,9},{9,8},{10,11... | collective-permute-start | bytes 1572872 | tf_op jit(solution)/shard_map/ppermute | solution.py:296
  3.1 44.8 %copy-start.1 = (s32[1,1,256]{2,1,0:T(1,128)S(1)}, s32[1,1,256]{2,1,0:T(1,128)}, u32[]{:S(2)}) copy-start(s32[1,1,256]{2,1,0:T(1,128)} %param.7) | copy-start | bytes 3076
  3.1 44.8 %copy-start.2 = (f32[1,1,256]{2,1,0:T(1,128)S(1)}, f32[1,1,256]{2,1,0:T(1,128)}, u32[]{:S(2)}) copy-start(f32[1,1,256]{2,1,0:T(1,128)} %param.8) | copy-start | bytes 3076
  47.9 3.5 %copy-start = (bf16[1,1,256,1024]{3,2,1,0:T(8,128)(2,1)S(1)}, bf16[1,1,256,1024]{3,2,1,0:T(8,128)(2,1)}, u32[]{:S(2)}) copy-start(bf16[1,1,256,1024]{3,2,1,0:T(8,128)(2,1)} %param.9) | copy-start | bytes 1572868
  47.9 3.5 %copy-start.3 = (s32[1,2]{1,0:T(1,128)S(1)}, s32[1,2]{1,0:T(1,128)}, u32[]{:S(2)}) copy-start(s32[1,2]{1,0:T(1,128)} %kinds_ref.1) | copy-start | bytes 28
  47.9 3.5 %copy-start.4 = (s32[1,2]{1,0:T(1,128)S(1)}, s32[1,2]{1,0:T(1,128)}, u32[]{:S(2)}) copy-start(s32[1,2]{1,0:T(1,128)} %groups_ref.1) | copy-start | bytes 28
  49.3 2.1 %collective-permute-start.1 = (bf16[256,1152]{1,0:T(8,128)(2,1)S(1)}, bf16[256,1152]{1,0:T(8,128)(2,1)S(1)}, u32[]{:S(2)}, u32[]{:S(2)}) collective-permute-start(bf16[256,1152]{1,0:T(8,128)(2,1)S(1)} %get-tuple-element.11.own_ref), channel_id=1, source_target_pairs={{0,1},{1,0},{2,3},{3,2},{4,5},{5,4},{6,7},{7,6},{8,9},{9,8},{10,11... | collective-permute-start | bytes 1769480 | tf_op jit(solution)/shard_map/ppermute | solution.py:334

commit v5 on v4

--- a/solution.py
+++ b/solution.py
@@ -12,7 +12,7 @@
 COLUMNS = 512
 MIB = 1024 * 1024
 
-STRIDE = 13
+STRIDE = 21
 
 f32 = jnp.float32
 bf16 = jnp.bfloat16

time: 94.2 us -> 93.3 us (level)
  blocking collectives: 78.9 us -> 77.9 us
    all_to_all x2, blocking collectives: 78.9 us -> 77.9 us  [exchange(): lax.all_to_all(value, 'member', split_axis=0, concat_axis=0, axis_index_g...]
where the time goes in v5:
time: 93.3 us; the launch traced here: 93 us
  blocking collectives  77.9 us (83%)
  Pallas kernels  12.9 us (14%)
  waiting for transfers between devices  1.99 us (2%)
    all_to_all x2, blocking collectives, exchange(): lax.all_to_all(value, 'member', split_axis=0, concat_axis=0, axis_index_g...  77.9 us
    pallas_call x1, Pallas kernels, shards(): pl.pallas_call(analyse, in_specs=[pl.BlockSpec(memory_space=pltpu.SMEM)]...  6.09 us
    pallas_call x1, Pallas kernels, shards(): pl.pallas_call(pack_members, in_specs=[pl.BlockSpec(memory_space=pltpu.HB...  3.12 us
    pallas_call x1, Pallas kernels, shards(): pl.pallas_call(unpack_members, in_specs=[pl.BlockSpec(memory_space=pltpu....  2.29 us
    ppermute x1, waiting for transfers between devices, shards(): other_seen = lax.ppermute(seen, 'region', swap)  1.99 us
  transfers between devices with their start and end apart: 2, of which 1 were waited for; matrix products, arithmetic and copies ran while one was open for 0% of the time, Pallas kernels for 3%

profile of v5, /device:TPU:0, one launch (start us, length us, event | category | flops | bytes accessed | tf_op | source)
XLA Modules:
  0.0 93.0 jit_solution(14270239453488006765)
XLA Ops:
  0.0 0.0 collective-permute-start
  0.0 3.1 %pack_members.1 = bf16[64,16,1152]{2,1,0:T(8,128)(2,1)S(1)} custom-call(f32[16,64,8,128]{3,2,1,0:T(8,128)} %bitcast.9), custom_call_target="tpu_custom_call" | custom-call | flops 4194304 | bytes 7340032 | tf_op jit(solution)/shard_map/pack_members/pallas_call | solution.py:298
  3.1 0.0 copy-start.1
  3.1 0.0 copy-start.2
  3.2 0.0 collective-permute-done.other_noise_ref
  3.2 44.6 %all_to_all.10.x_ref = bf16[64,16,1152]{2,1,0:T(8,128)(2,1)S(1)} all-to-all(bf16[64,16,1152]{2,1,0:T(8,128)(2,1)S(1)} %pack_members.1), channel_id=1, replica_groups={{0,42,84,126,40,82,124,38,80,122,36,78,120,34,76,118,32,74,116,30,72,11..., dimensions={0} | all-to-all | bytes 4718592 | tf_op jit(solution)/shard_map/all_to_all | solution.py:34
  47.8 0.0 copy-start
  47.8 0.0 copy-start.3
  47.8 0.0 copy-start.4
  47.8 0.0 copy-done.1
  47.8 0.0 copy-done.2
  47.8 1.4 %observe.1 = (bf16[1024,1024]{1,0:T(8,128)(2,1)S(1)}, bf16[256,1152]{1,0:T(8,128)(2,1)S(1)}) custom-call(bf16[64,16,1152]{2,1,0:T(8,128)(2,1)S(1)} %all_to_all.10.x_ref, s32[1,256]{1,0:T(1,128)S(1)} %bitcast.7, f32[1,256]{1,0:T(1,128)S(1)} %bitcast.8), custom_call_target="tpu_custom_call" | custom-call | tf_op jit(solution)/shard_map/observe/pallas_call | solution.py:317
  49.2 0.1 collective-permute-start.1
  49.3 2.0 %collective-permute-done.1.other_ref = bf16[256,1152]{1,0:T(8,128)(2,1)S(1)} collective-permute-done((bf16[256,1152]{1,0:T(8,128)(2,1)S(1)}, bf16[256,1152]{1,0:T(8,128)(2,1)S(1)}, u32[]{:S(2)}, u32[]{:S(2)}) %collective-permute-start.1) | collective-permute-done | bytes 589856 | tf_op jit(solution)/shard_map/ppermute | solution.py:334
  51.3 0.0 copy-done
  51.3 0.0 copy-done.3
  51.3 0.0 copy-done.4
  51.3 6.1 %analyse.1 = bf16[64,16,1024]{2,1,0:T(8,128)(2,1)S(1)} custom-call(s32[1,2]{1,0:T(1,128)S(1)} %copy-done.3, s32[1,2]{1,0:T(1,128)S(1)} %copy-done.4, bf16[1024,1024]{1,0:T(8,128)(2,1)S(1)} %get-tuple-element.10.anomaly_ref, bf16[256,1152]{1,0:T(8,128)(2,1)S(1)} %get-tuple-element.11.own_ref, bf16[256,1152]{1,0:T(8,128)(2,1)S(1)} %collective-permute-done.1.other_ref, ...), custom_call_target="tpu_custom_call" | custom-call | tf_op jit(solution)/shard_map/analyse/pallas_call | solution.py:336
  57.4 33.3 %all_to_all.11.x_ref = bf16[64,16,1024]{2,1,0:T(8,128)(2,1)S(1)} all-to-all(bf16[64,16,1024]{2,1,0:T(8,128)(2,1)S(1)} %analyse.1), channel_id=1, replica_groups={{0,42,84,126,40,82,124,38,80,122,36,78,120,34,76,118,32,74,116,30,72,11..., dimensions={0} | all-to-all | bytes 4194304 | tf_op jit(solution)/shard_map/all_to_all | solution.py:34
  90.7 2.3 %unpack_members.1 = f32[16,64,8,128]{3,2,1,0:T(8,128)} custom-call(bf16[64,16,1024]{2,1,0:T(8,128)(2,1)S(1)} %all_to_all.11.x_ref), custom_call_target="tpu_custom_call" | custom-call | tf_op jit(solution)/shard_map/unpack_members/pallas_call | solution.py:357
Async XLA Ops:
  0.0 3.2 %collective-permute-start = (bf16[256,1024]{1,0:T(8,128)(2,1)}, bf16[256,1024]{1,0:T(8,128)(2,1)S(1)}, u32[]{:S(2)}, u32[]{:S(2)}) collective-permute-start(bf16[256,1024]{1,0:T(8,128)(2,1)} %bitcast.5), channel_id=1, source_target_pairs={{0,1},{1,0},{2,3},{3,2},{4,5},{5,4},{6,7},{7,6},{8,9},{9,8},{10,11... | collective-permute-start | bytes 1572872 | tf_op jit(solution)/shard_map/ppermute | solution.py:296
  3.1 44.7 %copy-start.1 = (s32[1,1,256]{2,1,0:T(1,128)S(1)}, s32[1,1,256]{2,1,0:T(1,128)}, u32[]{:S(2)}) copy-start(s32[1,1,256]{2,1,0:T(1,128)} %param.7) | copy-start | bytes 3076
  3.1 44.7 %copy-start.2 = (f32[1,1,256]{2,1,0:T(1,128)S(1)}, f32[1,1,256]{2,1,0:T(1,128)}, u32[]{:S(2)}) copy-start(f32[1,1,256]{2,1,0:T(1,128)} %param.8) | copy-start | bytes 3076
  47.8 3.5 %copy-start = (bf16[1,1,256,1024]{3,2,1,0:T(8,128)(2,1)S(1)}, bf16[1,1,256,1024]{3,2,1,0:T(8,128)(2,1)}, u32[]{:S(2)}) copy-start(bf16[1,1,256,1024]{3,2,1,0:T(8,128)(2,1)} %param.9) | copy-start | bytes 1572868
  47.8 3.5 %copy-start.3 = (s32[1,2]{1,0:T(1,128)S(1)}, s32[1,2]{1,0:T(1,128)}, u32[]{:S(2)}) copy-start(s32[1,2]{1,0:T(1,128)} %kinds_ref.1) | copy-start | bytes 28
  47.8 3.5 %copy-start.4 = (s32[1,2]{1,0:T(1,128)S(1)}, s32[1,2]{1,0:T(1,128)}, u32[]{:S(2)}) copy-start(s32[1,2]{1,0:T(1,128)} %groups_ref.1) | copy-start | bytes 28
  49.2 2.1 %collective-permute-start.1 = (bf16[256,1152]{1,0:T(8,128)(2,1)S(1)}, bf16[256,1152]{1,0:T(8,128)(2,1)S(1)}, u32[]{:S(2)}, u32[]{:S(2)}) collective-permute-start(bf16[256,1152]{1,0:T(8,128)(2,1)S(1)} %get-tuple-element.11.own_ref), channel_id=1, source_target_pairs={{0,1},{1,0},{2,3},{3,2},{4,5},{5,4},{6,7},{7,6},{8,9},{9,8},{10,11... | collective-permute-start | bytes 1769480 | tf_op jit(solution)/shard_map/ppermute | solution.py:334

commit v6 on v5

--- a/solution.py
+++ b/solution.py
@@ -171,11 +171,23 @@
         ).astype(bf16)
 
 
+def own_part(anomaly_ref, own_ref, gain_ref, covariance_ref):
+    total_members = anomaly_ref.shape[0]
+    count = total_members - 1
+    rows = own_ref[:, :total_members]
+    cross = jnp.dot(rows, anomaly_ref[...], preferred_element_type=f32)
+    gain_ref[...] = (cross * (f32(1.0) / count)).astype(bf16)
+    product = lax.dot_general(rows, rows, (((1,), (1,)), ((), ())), preferred_element_type=f32)
+    covariance_ref[...] = (product * (f32(1.0) / count)).astype(bf16)
+
+
 def analyse(
     kinds_ref,
     groups_ref,
     anomaly_ref,
     own_ref,
+    own_gain_ref,
+    own_covariance_ref,
     other_ref,
     own_noise_ref,
     other_noise_ref,
@@ -204,15 +216,15 @@
     seen[tile:, :] = other_ref[:, :total_members]
     in_own = lax.broadcasted_iota(jnp.int32, (rows, 1), 0) < tile
     variance = jnp.where(in_own, own_variance, other_variance)
-    weight_rows = jnp.where(in_own, f32(1.0), cross_weight)
 
     product = lax.dot_general(
-        seen[...], seen[...], (((1,), (1,)), ((), ())), preferred_element_type=f32
+        seen[...], seen[tile:, :], (((1,), (1,)), ((), ())), preferred_element_type=f32
     )
-    for half in range(2):
-        columns = slice(half * tile, (half + 1) * tile)
-        weight = jnp.where(in_own == (half == 0), f32(1.0), cross_weight)
-        covariance[:, columns] = (product[:, columns] * (weight / count)).astype(bf16)
+    covariance[:tile, :tile] = own_covariance_ref[...]
+    between = product[:tile, :] * (cross_weight / count)
+    covariance[:tile, tile:] = between.astype(bf16)
+    covariance[tile:, :tile] = jnp.transpose(between).astype(bf16)
+    covariance[tile:, tile:] = (product[tile:, :] * (f32(1.0) / count)).astype(bf16)
     bound = variance + jnp.sum(jnp.abs(covariance[...].astype(f32)), axis=1, keepdims=True)
     largest = jnp.max(bound)
     lowest = jnp.minimum(own_variance, other_variance)
@@ -272,8 +284,9 @@
             - reach * apply(two_steps, span)
         ).astype(bf16)
 
-    cross = jnp.dot(seen[...], anomaly_ref[...], preferred_element_type=f32)
-    gain[...] = (cross * (weight_rows / count)).astype(bf16)
+    gain[:tile, :] = own_gain_ref[...]
+    cross = jnp.dot(seen[tile:, :], anomaly_ref[...], preferred_element_type=f32)
+    gain[tile:, :] = (cross * (cross_weight / count)).astype(bf16)
     increment = lax.dot_general(
         solved[...], gain[...], (((0,), (0,)), ((), ())), preferred_element_type=f32
     ).astype(bf16)
@@ -333,10 +346,25 @@
 
     other_seen = lax.ppermute(seen, "region", swap)
 
+    own_gain, own_covariance = pl.pallas_call(
+        own_part,
+        in_specs=[pl.BlockSpec(memory_space=pltpu.VMEM)] * 2,
+        out_specs=[pl.BlockSpec(memory_space=pltpu.VMEM)] * 2,
+        out_shape=[
+            jax.ShapeDtypeStruct((tile, cells), bf16),
+            jax.ShapeDtypeStruct((tile, tile), bf16),
+        ],
+        cost_estimate=pl.CostEstimate(
+            flops=2 * tile * total * (cells + tile), bytes_accessed=8 * MIB, transcendentals=0
+        ),
+        compiler_params=pltpu.CompilerParams(vmem_limit_bytes=12 * MIB),
+        name="own_part",
+    )(anomaly, seen)
+
     increment = pl.pallas_call(
         analyse,
         in_specs=[pl.BlockSpec(memory_space=pltpu.SMEM)] * 2
-        + [pl.BlockSpec(memory_space=pltpu.VMEM)] * 5,
+        + [pl.BlockSpec(memory_space=pltpu.VMEM)] * 7,
         out_specs=pl.BlockSpec(memory_space=pltpu.VMEM),
         out_shape=jax.ShapeDtypeStruct((bands, members, cells), bf16),
         scratch_shapes=[
@@ -350,7 +378,17 @@
         ],
         compiler_params=pltpu.CompilerParams(vmem_limit_bytes=28 * MIB),
         name="analyse",
-    )(noise_kind, taper_set, anomaly, seen, other_seen, own_noise, other_noise)
+    )(
+        noise_kind,
+        taper_set,
+        anomaly,
+        seen,
+        own_gain,
+        own_covariance,
+        other_seen,
+        own_noise,
+        other_noise,
+    )
 
     returned = exchange(increment)
 

time: 93.3 us -> 93.1 us (level)
  transfers between devices with their start and end apart: 2 -> 2, of which waited for: 1 -> 1; matrix products, arithmetic and copies ran while one was open for 0% -> 0% of each run, Pallas kernels for 3% -> 4%
where the time goes in v6:
time: 93.1 us; the launch traced here: 92.8 us
  blocking collectives  77.9 us (84%)
  Pallas kernels  13.6 us (15%)
  waiting for transfers between devices  1.13 us (1%)
    all_to_all x2, blocking collectives, exchange(): lax.all_to_all(value, 'member', split_axis=0, concat_axis=0, axis_index_g...  77.9 us
    pallas_call x1, Pallas kernels, shards(): pl.pallas_call(analyse, in_specs=[pl.BlockSpec(memory_space=pltpu.SMEM)]...  5.92 us
    pallas_call x1, Pallas kernels, shards(): pl.pallas_call(pack_members, in_specs=[pl.BlockSpec(memory_space=pltpu.HB...  3.12 us
    pallas_call x1, Pallas kernels, shards(): pl.pallas_call(unpack_members, in_specs=[pl.BlockSpec(memory_space=pltpu....  2.29 us
  transfers between devices with their start and end apart: 2, of which 1 were waited for; matrix products, arithmetic and copies ran while one was open for 0% of the time, Pallas kernels for 4%

profile of v6, /device:TPU:0, one launch (start us, length us, event | category | flops | bytes accessed | tf_op | source)
XLA Modules:
  0.0 92.8 jit_solution(16803609688528773781)
XLA Ops:
  0.0 0.0 collective-permute-start
  0.0 3.1 %pack_members.1 = bf16[64,16,1152]{2,1,0:T(8,128)(2,1)S(1)} custom-call(f32[16,64,8,128]{3,2,1,0:T(8,128)} %bitcast.9), custom_call_target="tpu_custom_call" | custom-call | flops 4194304 | bytes 7340032 | tf_op jit(solution)/shard_map/pack_members/pallas_call | solution.py:311
  3.1 0.0 copy-start.1
  3.1 0.0 copy-start.2
  3.2 0.0 collective-permute-done.other_noise_ref
  3.2 44.6 %all_to_all.10.x_ref = bf16[64,16,1152]{2,1,0:T(8,128)(2,1)S(1)} all-to-all(bf16[64,16,1152]{2,1,0:T(8,128)(2,1)S(1)} %pack_members.1), channel_id=1, replica_groups={{0,42,84,126,40,82,124,38,80,122,36,78,120,34,76,118,32,74,116,30,72,11..., dimensions={0} | all-to-all | bytes 4718592 | tf_op jit(solution)/shard_map/all_to_all | solution.py:34
  47.8 0.0 copy-done.1
  47.8 0.0 copy-done.2
  47.8 0.0 copy-start
  47.8 0.0 copy-start.3
  47.8 0.0 copy-start.4
  47.8 1.4 %observe.1 = (bf16[1024,1024]{1,0:T(8,128)(2,1)S(1)}, bf16[256,1152]{1,0:T(8,128)(2,1)S(1)}) custom-call(bf16[64,16,1152]{2,1,0:T(8,128)(2,1)S(1)} %all_to_all.10.x_ref, s32[1,256]{1,0:T(1,128)S(1)} %bitcast.7, f32[1,256]{1,0:T(1,128)S(1)} %bitcast.8), custom_call_target="tpu_custom_call" | custom-call | tf_op jit(solution)/shard_map/observe/pallas_call | solution.py:330
  49.3 0.1 collective-permute-start.1
  49.3 0.9 own_part.1
  50.2 1.1 %collective-permute-done.1.other_ref = bf16[256,1152]{1,0:T(8,128)(2,1)S(1)} collective-permute-done((bf16[256,1152]{1,0:T(8,128)(2,1)S(1)}, bf16[256,1152]{1,0:T(8,128)(2,1)S(1)}, u32[]{:S(2)}, u32[]{:S(2)}) %collective-permute-start.1) | collective-permute-done | bytes 589856 | tf_op jit(solution)/shard_map/ppermute | solution.py:347
  51.3 0.0 copy-done
  51.3 0.0 copy-done.3
  51.3 0.0 copy-done.4
  51.3 5.9 %analyse.1 = bf16[64,16,1024]{2,1,0:T(8,128)(2,1)S(1)} custom-call(s32[1,2]{1,0:T(1,128)S(1)} %copy-done.3, s32[1,2]{1,0:T(1,128)S(1)} %copy-done.4, bf16[1024,1024]{1,0:T(8,128)(2,1)S(1)} %get-tuple-element.12.anomaly_ref, bf16[256,1152]{1,0:T(8,128)(2,1)S(1)} %get-tuple-element.13.own_ref, bf16[256,1024]{1,0:T(8,128)(2,1)S(1)} %get-tuple-element.14.own_gain_ref, ...), custom_call_target="tpu_custom_call" | custom-call | tf_op jit(solution)/shard_map/analyse/pallas_call | solution.py:364
  57.3 33.3 %all_to_all.11.x_ref = bf16[64,16,1024]{2,1,0:T(8,128)(2,1)S(1)} all-to-all(bf16[64,16,1024]{2,1,0:T(8,128)(2,1)S(1)} %analyse.1), channel_id=1, replica_groups={{0,42,84,126,40,82,124,38,80,122,36,78,120,34,76,118,32,74,116,30,72,11..., dimensions={0} | all-to-all | bytes 4194304 | tf_op jit(solution)/shard_map/all_to_all | solution.py:34
  90.5 2.3 %unpack_members.1 = f32[16,64,8,128]{3,2,1,0:T(8,128)} custom-call(bf16[64,16,1024]{2,1,0:T(8,128)(2,1)S(1)} %all_to_all.11.x_ref), custom_call_target="tpu_custom_call" | custom-call | tf_op jit(solution)/shard_map/unpack_members/pallas_call | solution.py:395
Async XLA Ops:
  0.0 3.2 %collective-permute-start = (bf16[256,1024]{1,0:T(8,128)(2,1)}, bf16[256,1024]{1,0:T(8,128)(2,1)S(1)}, u32[]{:S(2)}, u32[]{:S(2)}) collective-permute-start(bf16[256,1024]{1,0:T(8,128)(2,1)} %bitcast.5), channel_id=1, source_target_pairs={{0,1},{1,0},{2,3},{3,2},{4,5},{5,4},{6,7},{7,6},{8,9},{9,8},{10,11... | collective-permute-start | bytes 1572872 | tf_op jit(solution)/shard_map/ppermute | solution.py:309
  3.1 44.7 %copy-start.1 = (s32[1,1,256]{2,1,0:T(1,128)S(1)}, s32[1,1,256]{2,1,0:T(1,128)}, u32[]{:S(2)}) copy-start(s32[1,1,256]{2,1,0:T(1,128)} %param.7) | copy-start | bytes 3076
  3.1 44.7 %copy-start.2 = (f32[1,1,256]{2,1,0:T(1,128)S(1)}, f32[1,1,256]{2,1,0:T(1,128)}, u32[]{:S(2)}) copy-start(f32[1,1,256]{2,1,0:T(1,128)} %param.8) | copy-start | bytes 3076
  47.8 3.5 %copy-start = (bf16[1,1,256,1024]{3,2,1,0:T(8,128)(2,1)S(1)}, bf16[1,1,256,1024]{3,2,1,0:T(8,128)(2,1)}, u32[]{:S(2)}) copy-start(bf16[1,1,256,1024]{3,2,1,0:T(8,128)(2,1)} %param.9) | copy-start | bytes 1572868
  47.8 3.5 %copy-start.3 = (s32[1,2]{1,0:T(1,128)S(1)}, s32[1,2]{1,0:T(1,128)}, u32[]{:S(2)}) copy-start(s32[1,2]{1,0:T(1,128)} %kinds_ref.1) | copy-start | bytes 28
  47.8 3.5 %copy-start.4 = (s32[1,2]{1,0:T(1,128)S(1)}, s32[1,2]{1,0:T(1,128)}, u32[]{:S(2)}) copy-start(s32[1,2]{1,0:T(1,128)} %groups_ref.1) | copy-start | bytes 28
  49.3 2.1 %collective-permute-start.1 = (bf16[256,1152]{1,0:T(8,128)(2,1)S(1)}, bf16[256,1152]{1,0:T(8,128)(2,1)S(1)}, u32[]{:S(2)}, u32[]{:S(2)}) collective-permute-start(bf16[256,1152]{1,0:T(8,128)(2,1)S(1)} %get-tuple-element.13.own_ref), channel_id=1, source_target_pairs={{0,1},{1,0},{2,3},{3,2},{4,5},{5,4},{6,7},{7,6},{8,9},{9,8},{10,11... | collective-permute-start | bytes 1769480 | tf_op jit(solution)/shard_map/ppermute | solution.py:347

commit v7 on v6

--- a/solution.py
+++ b/solution.py
@@ -10,6 +10,7 @@
 LANES = 128
 GROUPS = 8
 COLUMNS = 512
+SOLVE_COLUMNS = 256
 MIB = 1024 * 1024
 
 STRIDE = 21
@@ -238,7 +239,7 @@
     other_base = jnp.sum(other_ref[:, total_members:].astype(f32)[:, :3], axis=1, keepdims=True)
     own_scale = jnp.sqrt(jnp.full((1, 1), own_variance, f32))
     other_scale = jnp.sqrt(jnp.full((1, 1), other_variance, f32))
-    width = COLUMNS
+    width = SOLVE_COLUMNS
 
     steps = []
     reach_before, keep_before = 1.0 / center, f32(0.0)
@@ -251,7 +252,32 @@
         rho, reach_before, keep_before = rho_next, reach, keep
     inverse = 1.0 / center
 
-    spans = [slice(start, start + width) for start in range(0, total_members, width)]
+    spans = [slice(left, left + width) for left in range(0, total_members, width)]
+    devices, members, _ = out_ref.shape
+    places = place_of(devices)
+
+    def apply(held, span):
+        return jnp.dot(
+            covariance[...], held[:, span].astype(bf16), preferred_element_type=f32
+        )
+
+    def settle(span):
+        ahead, back, reach = steps[2]
+        solved[:, span] = (
+            (1.0 + ahead) * two_steps[:, span]
+            + (1.0 - back) * one_step[:, span]
+            + zero[:, span]
+            - reach * apply(two_steps, span)
+        ).astype(bf16)
+
+    def finish(span):
+        part = lax.dot_general(
+            solved[:, span], gain[...], (((0,), (0,)), ((), ())), preferred_element_type=f32
+        ).astype(bf16)
+        for device in range(span.start // members, span.stop // members):
+            first = device * members - span.start
+            out_ref[places[device]] = part[first : first + members]
+
     for span in spans:
         zero[:tile, span] = inverse * (
             own_base + own_scale * own_noise_ref[:, span].astype(f32) - own_ref[:, span].astype(f32)
@@ -261,12 +287,9 @@
             + other_scale * other_noise_ref[:, span].astype(f32)
             - other_ref[:, span].astype(f32)
         )
-
-    def apply(held, span):
-        return jnp.dot(
-            covariance[...], held[:, span].astype(bf16), preferred_element_type=f32
-        )
-
+    gain[:tile, :] = own_gain_ref[...]
+    cross = jnp.dot(seen[tile:, :], anomaly_ref[...], preferred_element_type=f32)
+    gain[tile:, :] = (cross * (cross_weight / count)).astype(bf16)
     for span in spans:
         ahead, _, reach = steps[0]
         one_step[:, span] = ahead * zero[:, span] - reach * apply(zero, span)
@@ -275,24 +298,11 @@
         two_steps[:, span] = (
             ahead * one_step[:, span] - back * zero[:, span] - reach * apply(one_step, span)
         )
-    for span in spans:
-        ahead, back, reach = steps[2]
-        solved[:, span] = (
-            (1.0 + ahead) * two_steps[:, span]
-            + (1.0 - back) * one_step[:, span]
-            + zero[:, span]
-            - reach * apply(two_steps, span)
-        ).astype(bf16)
-
-    gain[:tile, :] = own_gain_ref[...]
-    cross = jnp.dot(seen[tile:, :], anomaly_ref[...], preferred_element_type=f32)
-    gain[tile:, :] = (cross * (cross_weight / count)).astype(bf16)
-    increment = lax.dot_general(
-        solved[...], gain[...], (((0,), (0,)), ((), ())), preferred_element_type=f32
-    ).astype(bf16)
-    devices, members, _ = out_ref.shape
-    for device, place in enumerate(place_of(devices)):
-        out_ref[place] = increment[device * members : (device + 1) * members]
+    settle(spans[0])
+    for span, later in zip(spans, spans[1:]):
+        settle(later)
+        finish(span)
+    finish(spans[-1])
 
 
 def shards(

time: 93.1 us -> 92.2 us (level)
    pallas_call x1, Pallas kernels: 5.92 us -> 4.96 us  [shards(): pl.pallas_call(analyse, in_specs=[pl.BlockSpec(memory_space=pltpu.SMEM)]...]
where the time goes in v7:
time: 92.2 us; the launch traced here: 91.9 us
  blocking collectives  77.9 us (84%)
  Pallas kernels  12.7 us (14%)
  waiting for transfers between devices  1.13 us (1%)
    all_to_all x2, blocking collectives, exchange(): lax.all_to_all(value, 'member', split_axis=0, concat_axis=0, axis_index_g...  77.9 us
    pallas_call x1, Pallas kernels, shards(): pl.pallas_call(analyse, in_specs=[pl.BlockSpec(memory_space=pltpu.SMEM)]...  4.96 us
    pallas_call x1, Pallas kernels, shards(): pl.pallas_call(pack_members, in_specs=[pl.BlockSpec(memory_space=pltpu.HB...  3.12 us
    pallas_call x1, Pallas kernels, shards(): pl.pallas_call(unpack_members, in_specs=[pl.BlockSpec(memory_space=pltpu....  2.29 us
  transfers between devices with their start and end apart: 2, of which 1 were waited for; matrix products, arithmetic and copies ran while one was open for 0% of the time, Pallas kernels for 4%

profile of v7, /device:TPU:0, one launch (start us, length us, event | category | flops | bytes accessed | tf_op | source)
XLA Modules:
  0.0 91.9 jit_solution(8095600218608876142)
XLA Ops:
  0.0 0.0 collective-permute-start
  0.0 3.1 %pack_members.1 = bf16[64,16,1152]{2,1,0:T(8,128)(2,1)S(1)} custom-call(f32[16,64,8,128]{3,2,1,0:T(8,128)} %bitcast.9), custom_call_target="tpu_custom_call" | custom-call | flops 4194304 | bytes 7340032 | tf_op jit(solution)/shard_map/pack_members/pallas_call | solution.py:321
  3.1 0.0 copy-start.1
  3.1 0.0 copy-start.2
  3.2 0.0 collective-permute-done.other_noise_ref
  3.2 44.6 %all_to_all.10.x_ref = bf16[64,16,1152]{2,1,0:T(8,128)(2,1)S(1)} all-to-all(bf16[64,16,1152]{2,1,0:T(8,128)(2,1)S(1)} %pack_members.1), channel_id=1, replica_groups={{0,42,84,126,40,82,124,38,80,122,36,78,120,34,76,118,32,74,116,30,72,11..., dimensions={0} | all-to-all | bytes 4718592 | tf_op jit(solution)/shard_map/all_to_all | solution.py:35
  47.8 0.0 copy-done.1
  47.8 0.0 copy-done.2
  47.8 0.0 copy-start
  47.8 0.0 copy-start.3
  47.8 0.0 copy-start.4
  47.8 1.4 %observe.1 = (bf16[1024,1024]{1,0:T(8,128)(2,1)S(1)}, bf16[256,1152]{1,0:T(8,128)(2,1)S(1)}) custom-call(bf16[64,16,1152]{2,1,0:T(8,128)(2,1)S(1)} %all_to_all.10.x_ref, s32[1,256]{1,0:T(1,128)S(1)} %bitcast.7, f32[1,256]{1,0:T(1,128)S(1)} %bitcast.8), custom_call_target="tpu_custom_call" | custom-call | tf_op jit(solution)/shard_map/observe/pallas_call | solution.py:340
  49.3 0.1 collective-permute-start.1
  49.3 0.9 own_part.1
  50.2 1.1 %collective-permute-done.1.other_ref = bf16[256,1152]{1,0:T(8,128)(2,1)S(1)} collective-permute-done((bf16[256,1152]{1,0:T(8,128)(2,1)S(1)}, bf16[256,1152]{1,0:T(8,128)(2,1)S(1)}, u32[]{:S(2)}, u32[]{:S(2)}) %collective-permute-start.1) | collective-permute-done | bytes 589856 | tf_op jit(solution)/shard_map/ppermute | solution.py:357
  51.3 0.0 copy-done
  51.3 0.0 copy-done.3
  51.3 0.0 copy-done.4
  51.3 5.0 %analyse.1 = bf16[64,16,1024]{2,1,0:T(8,128)(2,1)S(1)} custom-call(s32[1,2]{1,0:T(1,128)S(1)} %copy-done.3, s32[1,2]{1,0:T(1,128)S(1)} %copy-done.4, bf16[1024,1024]{1,0:T(8,128)(2,1)S(1)} %get-tuple-element.12.anomaly_ref, bf16[256,1152]{1,0:T(8,128)(2,1)S(1)} %get-tuple-element.13.own_ref, bf16[256,1024]{1,0:T(8,128)(2,1)S(1)} %get-tuple-element.14.own_gain_ref, ...), custom_call_target="tpu_custom_call" | custom-call | tf_op jit(solution)/shard_map/analyse/pallas_call | solution.py:374
  56.3 33.3 %all_to_all.11.x_ref = bf16[64,16,1024]{2,1,0:T(8,128)(2,1)S(1)} all-to-all(bf16[64,16,1024]{2,1,0:T(8,128)(2,1)S(1)} %analyse.1), channel_id=1, replica_groups={{0,42,84,126,40,82,124,38,80,122,36,78,120,34,76,118,32,74,116,30,72,11..., dimensions={0} | all-to-all | bytes 4194304 | tf_op jit(solution)/shard_map/all_to_all | solution.py:35
  89.6 2.3 %unpack_members.1 = f32[16,64,8,128]{3,2,1,0:T(8,128)} custom-call(bf16[64,16,1024]{2,1,0:T(8,128)(2,1)S(1)} %all_to_all.11.x_ref), custom_call_target="tpu_custom_call" | custom-call | tf_op jit(solution)/shard_map/unpack_members/pallas_call | solution.py:405
Async XLA Ops:
  0.0 3.2 %collective-permute-start = (bf16[256,1024]{1,0:T(8,128)(2,1)}, bf16[256,1024]{1,0:T(8,128)(2,1)S(1)}, u32[]{:S(2)}, u32[]{:S(2)}) collective-permute-start(bf16[256,1024]{1,0:T(8,128)(2,1)} %bitcast.5), channel_id=1, source_target_pairs={{0,1},{1,0},{2,3},{3,2},{4,5},{5,4},{6,7},{7,6},{8,9},{9,8},{10,11... | collective-permute-start | bytes 1572872 | tf_op jit(solution)/shard_map/ppermute | solution.py:319
  3.1 44.7 %copy-start.1 = (s32[1,1,256]{2,1,0:T(1,128)S(1)}, s32[1,1,256]{2,1,0:T(1,128)}, u32[]{:S(2)}) copy-start(s32[1,1,256]{2,1,0:T(1,128)} %param.7) | copy-start | bytes 3076
  3.1 44.7 %copy-start.2 = (f32[1,1,256]{2,1,0:T(1,128)S(1)}, f32[1,1,256]{2,1,0:T(1,128)}, u32[]{:S(2)}) copy-start(f32[1,1,256]{2,1,0:T(1,128)} %param.8) | copy-start | bytes 3076
  47.8 3.5 %copy-start = (bf16[1,1,256,1024]{3,2,1,0:T(8,128)(2,1)S(1)}, bf16[1,1,256,1024]{3,2,1,0:T(8,128)(2,1)}, u32[]{:S(2)}) copy-start(bf16[1,1,256,1024]{3,2,1,0:T(8,128)(2,1)} %param.9) | copy-start | bytes 1572868
  47.8 3.5 %copy-start.3 = (s32[1,2]{1,0:T(1,128)S(1)}, s32[1,2]{1,0:T(1,128)}, u32[]{:S(2)}) copy-start(s32[1,2]{1,0:T(1,128)} %kinds_ref.1) | copy-start | bytes 28
  47.8 3.5 %copy-start.4 = (s32[1,2]{1,0:T(1,128)S(1)}, s32[1,2]{1,0:T(1,128)}, u32[]{:S(2)}) copy-start(s32[1,2]{1,0:T(1,128)} %groups_ref.1) | copy-start | bytes 28
  49.3 2.1 %collective-permute-start.1 = (bf16[256,1152]{1,0:T(8,128)(2,1)S(1)}, bf16[256,1152]{1,0:T(8,128)(2,1)S(1)}, u32[]{:S(2)}, u32[]{:S(2)}) collective-permute-start(bf16[256,1152]{1,0:T(8,128)(2,1)S(1)} %get-tuple-element.13.own_ref), channel_id=1, source_target_pairs={{0,1},{1,0},{2,3},{3,2},{4,5},{5,4},{6,7},{7,6},{8,9},{9,8},{10,11... | collective-permute-start | bytes 1769480 | tf_op jit(solution)/shard_map/ppermute | solution.py:357

commit v8 on v7

--- a/solution.py
+++ b/solution.py
@@ -172,7 +172,9 @@
         ).astype(bf16)
 
 
-def own_part(anomaly_ref, own_ref, gain_ref, covariance_ref):
+def own_part(
+    kinds_ref, anomaly_ref, own_ref, noise_ref, gain_ref, covariance_ref, innovation_ref
+):
     total_members = anomaly_ref.shape[0]
     count = total_members - 1
     rows = own_ref[:, :total_members]
@@ -180,6 +182,11 @@
     gain_ref[...] = (cross * (f32(1.0) / count)).astype(bf16)
     product = lax.dot_general(rows, rows, (((1,), (1,)), ((), ())), preferred_element_type=f32)
     covariance_ref[...] = (product * (f32(1.0) / count)).astype(bf16)
+    kind = kinds_ref[0, lax.axis_index("region")]
+    variance = 0.5 * lax.shift_left(jnp.int32(1), kind).astype(f32)
+    scale = jnp.sqrt(jnp.full((1, 1), variance, f32))
+    base = jnp.sum(own_ref[:, total_members:].astype(f32)[:, :3], axis=1, keepdims=True)
+    innovation_ref[...] = base + scale * noise_ref[...].astype(f32) - rows.astype(f32)
 
 
 def analyse(
@@ -190,7 +197,7 @@
     own_gain_ref,
     own_covariance_ref,
     other_ref,
-    own_noise_ref,
+    own_innovation_ref,
     other_noise_ref,
     out_ref,
     seen,
@@ -235,9 +242,7 @@
     sigma = center / radius
     rho = 1.0 / sigma
 
-    own_base = jnp.sum(own_ref[:, total_members:].astype(f32)[:, :3], axis=1, keepdims=True)
     other_base = jnp.sum(other_ref[:, total_members:].astype(f32)[:, :3], axis=1, keepdims=True)
-    own_scale = jnp.sqrt(jnp.full((1, 1), own_variance, f32))
     other_scale = jnp.sqrt(jnp.full((1, 1), other_variance, f32))
     width = SOLVE_COLUMNS
 
@@ -279,9 +284,7 @@
             out_ref[places[device]] = part[first : first + members]
 
     for span in spans:
-        zero[:tile, span] = inverse * (
-            own_base + own_scale * own_noise_ref[:, span].astype(f32) - own_ref[:, span].astype(f32)
-        )
+        zero[:tile, span] = inverse * own_innovation_ref[:, span]
         zero[tile:, span] = inverse * (
             other_base
             + other_scale * other_noise_ref[:, span].astype(f32)
@@ -356,20 +359,22 @@
 
     other_seen = lax.ppermute(seen, "region", swap)
 
-    own_gain, own_covariance = pl.pallas_call(
+    own_gain, own_covariance, own_innovation = pl.pallas_call(
         own_part,
-        in_specs=[pl.BlockSpec(memory_space=pltpu.VMEM)] * 2,
-        out_specs=[pl.BlockSpec(memory_space=pltpu.VMEM)] * 2,
+        in_specs=[pl.BlockSpec(memory_space=pltpu.SMEM)]
+        + [pl.BlockSpec(memory_space=pltpu.VMEM)] * 3,
+        out_specs=[pl.BlockSpec(memory_space=pltpu.VMEM)] * 3,
         out_shape=[
             jax.ShapeDtypeStruct((tile, cells), bf16),
             jax.ShapeDtypeStruct((tile, tile), bf16),
+            jax.ShapeDtypeStruct((tile, total), f32),
         ],
         cost_estimate=pl.CostEstimate(
             flops=2 * tile * total * (cells + tile), bytes_accessed=8 * MIB, transcendentals=0
         ),
         compiler_params=pltpu.CompilerParams(vmem_limit_bytes=12 * MIB),
         name="own_part",
-    )(anomaly, seen)
+    )(noise_kind, anomaly, seen, own_noise)
 
     increment = pl.pallas_call(
         analyse,
@@ -396,7 +401,7 @@
         own_gain,
         own_covariance,
         other_seen,
-        own_noise,
+        own_innovation,
         other_noise,
     )
 

time: 92.2 us -> 92.3 us (level)
  transfers between devices with their start and end apart: 2 -> 2, of which waited for: 1 -> 1; matrix products, arithmetic and copies ran while one was open for 0% -> 0% of each run, Pallas kernels for 4% -> 5%
where the time goes in v8:
time: 92.3 us; the launch traced here: 92 us
  blocking collectives  77.9 us (84%)
  Pallas kernels  13.4 us (15%)
    all_to_all x2, blocking collectives, exchange(): lax.all_to_all(value, 'member', split_axis=0, concat_axis=0, axis_index_g...  77.9 us
    pallas_call x1, Pallas kernels, shards(): pl.pallas_call(analyse, in_specs=[pl.BlockSpec(memory_space=pltpu.SMEM)]...  5.1 us
    pallas_call x1, Pallas kernels, shards(): pl.pallas_call(pack_members, in_specs=[pl.BlockSpec(memory_space=pltpu.HB...  3.12 us
    pallas_call x1, Pallas kernels, shards(): pl.pallas_call(unpack_members, in_specs=[pl.BlockSpec(memory_space=pltpu....  2.29 us
  transfers between devices with their start and end apart: 2, of which 1 were waited for; matrix products, arithmetic and copies ran while one was open for 0% of the time, Pallas kernels for 5%

profile of v8, /device:TPU:0, one launch (start us, length us, event | category | flops | bytes accessed | tf_op | source)
XLA Modules:
  0.0 92.0 jit_solution(7114481704738198321)
XLA Ops:
  0.0 0.0 collective-permute-start
  0.0 3.1 %pack_members.1 = bf16[64,16,1152]{2,1,0:T(8,128)(2,1)S(1)} custom-call(f32[16,64,8,128]{3,2,1,0:T(8,128)} %bitcast.9), custom_call_target="tpu_custom_call" | custom-call | flops 4194304 | bytes 7340032 | tf_op jit(solution)/shard_map/pack_members/pallas_call | solution.py:324
  3.1 0.0 copy-start.2
  3.1 0.0 copy-start.3
  3.2 0.0 collective-permute-done.other_noise_ref
  3.2 44.6 %all_to_all.10.x_ref = bf16[64,16,1152]{2,1,0:T(8,128)(2,1)S(1)} all-to-all(bf16[64,16,1152]{2,1,0:T(8,128)(2,1)S(1)} %pack_members.1), channel_id=1, replica_groups={{0,42,84,126,40,82,124,38,80,122,36,78,120,34,76,118,32,74,116,30,72,11..., dimensions={0} | all-to-all | bytes 4718592 | tf_op jit(solution)/shard_map/all_to_all | solution.py:35
  47.8 0.0 copy-start
  47.8 0.0 copy-start.1
  47.8 0.0 copy-done.2
  47.8 0.0 copy-done.3
  47.8 0.0 copy-start.4
  47.8 1.4 %observe.1 = (bf16[1024,1024]{1,0:T(8,128)(2,1)S(1)}, bf16[256,1152]{1,0:T(8,128)(2,1)S(1)}) custom-call(bf16[64,16,1152]{2,1,0:T(8,128)(2,1)S(1)} %all_to_all.10.x_ref, s32[1,256]{1,0:T(1,128)S(1)} %bitcast.7, f32[1,256]{1,0:T(1,128)S(1)} %bitcast.8), custom_call_target="tpu_custom_call" | custom-call | tf_op jit(solution)/shard_map/observe/pallas_call | solution.py:343
  49.2 0.1 collective-permute-start.1
  49.3 0.0 copy-done
  49.3 0.0 copy-done.1
  49.4 1.5 %own_part.1 = (bf16[256,1024]{1,0:T(8,128)(2,1)S(1)}, bf16[256,256]{1,0:T(8,128)(2,1)S(1)}, f32[256,1024]{1,0:T(8,128)S(1)}) custom-call(s32[1,2]{1,0:T(1,128)S(1)} %copy-done.1, bf16[1024,1024]{1,0:T(8,128)(2,1)S(1)} %get-tuple-element.13.anomaly_ref, bf16[256,1152]{1,0:T(8,128)(2,1)S(1)} %get-tuple-element.14.own_ref, bf16[256,1024]{1,0:T(8,128)(2,1)S(1)} %bitcast.6), custom_call_target="tpu_custom_call" | custom-call | flops 671088640 | bytes 8388608 | tf_op jit(solution)/shard_map/own_part/pallas_call | solution.py:362
  50.9 0.5 collective-permute-done.1.other_ref
  51.3 0.0 copy-done.4
  51.3 5.1 %analyse.1 = bf16[64,16,1024]{2,1,0:T(8,128)(2,1)S(1)} custom-call(s32[1,2]{1,0:T(1,128)S(1)} %copy-done.1, s32[1,2]{1,0:T(1,128)S(1)} %copy-done.4, bf16[1024,1024]{1,0:T(8,128)(2,1)S(1)} %get-tuple-element.13.anomaly_ref, bf16[256,1152]{1,0:T(8,128)(2,1)S(1)} %get-tuple-element.14.own_ref, bf16[256,1024]{1,0:T(8,128)(2,1)S(1)} %get-tuple-element.15.own_gain_ref, ...), custom_call_target="tpu_custom_call" | custom-call | tf_op jit(solution)/shard_map/analyse/pallas_call | solution.py:379
  56.4 33.3 %all_to_all.11.x_ref = bf16[64,16,1024]{2,1,0:T(8,128)(2,1)S(1)} all-to-all(bf16[64,16,1024]{2,1,0:T(8,128)(2,1)S(1)} %analyse.1), channel_id=1, replica_groups={{0,42,84,126,40,82,124,38,80,122,36,78,120,34,76,118,32,74,116,30,72,11..., dimensions={0} | all-to-all | bytes 4194304 | tf_op jit(solution)/shard_map/all_to_all | solution.py:35
  89.7 2.3 %unpack_members.1 = f32[16,64,8,128]{3,2,1,0:T(8,128)} custom-call(bf16[64,16,1024]{2,1,0:T(8,128)(2,1)S(1)} %all_to_all.11.x_ref), custom_call_target="tpu_custom_call" | custom-call | tf_op jit(solution)/shard_map/unpack_members/pallas_call | solution.py:410
Async XLA Ops:
  0.0 3.2 %collective-permute-start = (bf16[256,1024]{1,0:T(8,128)(2,1)}, bf16[256,1024]{1,0:T(8,128)(2,1)S(1)}, u32[]{:S(2)}, u32[]{:S(2)}) collective-permute-start(bf16[256,1024]{1,0:T(8,128)(2,1)} %bitcast.5), channel_id=1, source_target_pairs={{0,1},{1,0},{2,3},{3,2},{4,5},{5,4},{6,7},{7,6},{8,9},{9,8},{10,11... | collective-permute-start | bytes 1572872 | tf_op jit(solution)/shard_map/ppermute | solution.py:322
  3.1 44.7 %copy-start.2 = (s32[1,1,256]{2,1,0:T(1,128)S(1)}, s32[1,1,256]{2,1,0:T(1,128)}, u32[]{:S(2)}) copy-start(s32[1,1,256]{2,1,0:T(1,128)} %param.7) | copy-start | bytes 3076
  3.1 44.7 %copy-start.3 = (f32[1,1,256]{2,1,0:T(1,128)S(1)}, f32[1,1,256]{2,1,0:T(1,128)}, u32[]{:S(2)}) copy-start(f32[1,1,256]{2,1,0:T(1,128)} %param.8) | copy-start | bytes 3076
  47.8 1.5 %copy-start = (bf16[1,1,256,1024]{3,2,1,0:T(8,128)(2,1)S(1)}, bf16[1,1,256,1024]{3,2,1,0:T(8,128)(2,1)}, u32[]{:S(2)}) copy-start(bf16[1,1,256,1024]{3,2,1,0:T(8,128)(2,1)} %param.9) | copy-start | bytes 1572868
  47.8 1.6 %copy-start.1 = (s32[1,2]{1,0:T(1,128)S(1)}, s32[1,2]{1,0:T(1,128)}, u32[]{:S(2)}) copy-start(s32[1,2]{1,0:T(1,128)} %kinds_ref.3) | copy-start | bytes 28
  47.8 3.5 %copy-start.4 = (s32[1,2]{1,0:T(1,128)S(1)}, s32[1,2]{1,0:T(1,128)}, u32[]{:S(2)}) copy-start(s32[1,2]{1,0:T(1,128)} %groups_ref.1) | copy-start | bytes 28
  49.2 2.1 %collective-permute-start.1 = (bf16[256,1152]{1,0:T(8,128)(2,1)S(1)}, bf16[256,1152]{1,0:T(8,128)(2,1)S(1)}, u32[]{:S(2)}, u32[]{:S(2)}) collective-permute-start(bf16[256,1152]{1,0:T(8,128)(2,1)S(1)} %get-tuple-element.14.own_ref), channel_id=1, source_target_pairs={{0,1},{1,0},{2,3},{3,2},{4,5},{5,4},{6,7},{7,6},{8,9},{9,8},{10,11... | collective-permute-start | bytes 1769480 | tf_op jit(solution)/shard_map/ppermute | solution.py:360

commit v9 on v7

--- a/solution.py
+++ b/solution.py
@@ -316,7 +316,6 @@
     swap = [(0, 1), (1, 0)]
 
     own_noise = measurement_noise.reshape(tile, total)
-    other_noise = lax.ppermute(own_noise, "region", swap)
 
     packed = pl.pallas_call(
         pack_members,
@@ -334,8 +333,8 @@
         name="pack_members",
     )(prior_samples.reshape(members, bands, chunks, LANES))
 
-    packed, other_noise = lax.optimization_barrier((packed, other_noise))
-    arrived = exchange(packed)
+    arrived, own_noise = lax.optimization_barrier((exchange(packed), own_noise))
+    other_noise = lax.ppermute(own_noise, "region", swap)
 
     anomaly, seen = pl.pallas_call(
         observe,
@@ -350,10 +349,14 @@
             pltpu.VMEM((bands, chunks, LANES), f32),
             pltpu.VMEM((tile, cells), bf16),
         ],
+        cost_estimate=pl.CostEstimate(
+            flops=2 * tile * total * cells, bytes_accessed=8 * MIB, transcendentals=0
+        ),
         compiler_params=pltpu.CompilerParams(vmem_limit_bytes=12 * MIB),
         name="observe",
     )(arrived, measured_point.reshape(1, tile), measured_reading.reshape(1, tile))
 
+    seen, other_noise = lax.optimization_barrier((seen, other_noise))
     other_seen = lax.ppermute(seen, "region", swap)
 
     own_gain, own_covariance = pl.pallas_call(

time: 92.2 us -> 92 us (level)
  transfers between devices with their start and end apart: 2 -> 2, of which waited for: 1 -> 2; matrix products, arithmetic and copies ran while one was open for 0% -> 0% of each run, Pallas kernels for 4% -> 2%
where the time goes in v9:
time: 92 us; the launch traced here: 91.7 us
  blocking collectives  77.4 us (84%)
  Pallas kernels  12.6 us (14%)
  waiting for transfers between devices  1.45 us (2%)
    all_to_all x2, blocking collectives, exchange(): lax.all_to_all(value, 'member', split_axis=0, concat_axis=0, axis_index_g...  77.4 us
    pallas_call x1, Pallas kernels, shards(): pl.pallas_call(analyse, in_specs=[pl.BlockSpec(memory_space=pltpu.SMEM)]...  4.97 us
    pallas_call x1, Pallas kernels, shards(): pl.pallas_call(pack_members, in_specs=[pl.BlockSpec(memory_space=pltpu.HB...  3.12 us
    pallas_call x1, Pallas kernels, shards(): pl.pallas_call(unpack_members, in_specs=[pl.BlockSpec(memory_space=pltpu....  2.29 us
  transfers between devices with their start and end apart: 2, of which 2 were waited for; matrix products, arithmetic and copies ran while one was open for 0% of the time, Pallas kernels for 2%

profile of v9, /device:TPU:0, one launch (start us, length us, event | category | flops | bytes accessed | tf_op | source)
XLA Modules:
  0.0 91.7 jit_solution(13749332639504972708)
XLA Ops:
  0.0 3.1 %pack_members.1 = bf16[64,16,1152]{2,1,0:T(8,128)(2,1)S(1)} custom-call(f32[16,64,8,128]{3,2,1,0:T(8,128)} %bitcast.9), custom_call_target="tpu_custom_call" | custom-call | flops 4194304 | bytes 7340032 | tf_op jit(solution)/shard_map/pack_members/pallas_call | solution.py:320
  3.1 0.0 copy-start
  3.1 0.0 copy-start.1
  3.2 0.0 copy-start.2
  3.2 44.1 %all_to_all.10.x_ref = bf16[64,16,1152]{2,1,0:T(8,128)(2,1)S(1)} all-to-all(bf16[64,16,1152]{2,1,0:T(8,128)(2,1)S(1)} %pack_members.1), channel_id=1, replica_groups={{0,42,84,126,40,82,124,38,80,122,36,78,120,34,76,118,32,74,116,30,72,11..., dimensions={0} | all-to-all | bytes 4718592 | tf_op jit(solution)/shard_map/all_to_all | solution.py:35
  47.3 0.0 copy-done
  47.3 0.0 collective-permute-start
  47.3 0.0 copy-done.1
  47.3 0.0 copy-done.2
  47.3 0.0 copy-start.3
  47.3 0.0 copy-start.4
  47.3 1.4 %observe.1 = (bf16[1024,1024]{1,0:T(8,128)(2,1)S(1)}, bf16[256,1152]{1,0:T(8,128)(2,1)S(1)}) custom-call(bf16[64,16,1152]{2,1,0:T(8,128)(2,1)S(1)} %all_to_all.10.x_ref, s32[1,256]{1,0:T(1,128)S(1)} %bitcast.7, f32[1,256]{1,0:T(1,128)S(1)} %bitcast.8), custom_call_target="tpu_custom_call" | custom-call | flops 536870912 | bytes 8388608 | tf_op jit(solution)/shard_map/observe/pallas_call | solution.py:339
  48.7 0.4 collective-permute-done.other_noise_ref
  49.2 0.1 collective-permute-start.1
  49.3 0.9 own_part.1
  50.2 1.0 %collective-permute-done.1.other_ref = bf16[256,1152]{1,0:T(8,128)(2,1)S(1)} collective-permute-done((bf16[256,1152]{1,0:T(8,128)(2,1)S(1)}, bf16[256,1152]{1,0:T(8,128)(2,1)S(1)}, u32[]{:S(2)}, u32[]{:S(2)}) %collective-permute-start.1) | collective-permute-done | bytes 589856 | tf_op jit(solution)/shard_map/ppermute | solution.py:360
  51.2 0.0 copy-done.3
  51.2 0.0 copy-done.4
  51.2 5.0 %analyse.1 = bf16[64,16,1024]{2,1,0:T(8,128)(2,1)S(1)} custom-call(s32[1,2]{1,0:T(1,128)S(1)} %copy-done.3, s32[1,2]{1,0:T(1,128)S(1)} %copy-done.4, bf16[1024,1024]{1,0:T(8,128)(2,1)S(1)} %get-tuple-element.14.anomaly_ref, bf16[256,1152]{1,0:T(8,128)(2,1)S(1)} %get-tuple-element.17.own_ref, bf16[256,1024]{1,0:T(8,128)(2,1)S(1)} %get-tuple-element.18.own_gain_ref, ...), custom_call_target="tpu_custom_call" | custom-call | tf_op jit(solution)/shard_map/analyse/pallas_call | solution.py:377
  56.2 33.3 %all_to_all.11.x_ref = bf16[64,16,1024]{2,1,0:T(8,128)(2,1)S(1)} all-to-all(bf16[64,16,1024]{2,1,0:T(8,128)(2,1)S(1)} %analyse.1), channel_id=1, replica_groups={{0,42,84,126,40,82,124,38,80,122,36,78,120,34,76,118,32,74,116,30,72,11..., dimensions={0} | all-to-all | bytes 4194304 | tf_op jit(solution)/shard_map/all_to_all | solution.py:35
  89.5 2.3 %unpack_members.1 = f32[16,64,8,128]{3,2,1,0:T(8,128)} custom-call(bf16[64,16,1024]{2,1,0:T(8,128)(2,1)S(1)} %all_to_all.11.x_ref), custom_call_target="tpu_custom_call" | custom-call | tf_op jit(solution)/shard_map/unpack_members/pallas_call | solution.py:408
Async XLA Ops:
  3.1 44.1 %copy-start = (bf16[1,1,256,1024]{3,2,1,0:T(8,128)(2,1)S(1)}, bf16[1,1,256,1024]{3,2,1,0:T(8,128)(2,1)}, u32[]{:S(2)}) copy-start(bf16[1,1,256,1024]{3,2,1,0:T(8,128)(2,1)} %param.9) | copy-start | bytes 1572868
  3.1 44.1 %copy-start.1 = (s32[1,1,256]{2,1,0:T(1,128)S(1)}, s32[1,1,256]{2,1,0:T(1,128)}, u32[]{:S(2)}) copy-start(s32[1,1,256]{2,1,0:T(1,128)} %param.7) | copy-start | bytes 3076
  3.2 44.1 %copy-start.2 = (f32[1,1,256]{2,1,0:T(1,128)S(1)}, f32[1,1,256]{2,1,0:T(1,128)}, u32[]{:S(2)}) copy-start(f32[1,1,256]{2,1,0:T(1,128)} %param.8) | copy-start | bytes 3076
  47.3 1.9 %collective-permute-start = (bf16[256,1024]{1,0:T(8,128)(2,1)S(1)}, bf16[256,1024]{1,0:T(8,128)(2,1)S(1)}, u32[]{:S(2)}, u32[]{:S(2)}) collective-permute-start(bf16[256,1024]{1,0:T(8,128)(2,1)S(1)} %bitcast.5), channel_id=1, source_target_pairs={{0,1},{1,0},{2,3},{3,2},{4,5},{5,4},{6,7},{7,6},{8,9},{9,8},{10,11... | collective-permute-start | bytes 1572872 | tf_op jit(solution)/shard_map/ppermute | solution.py:337
  47.3 3.9 %copy-start.3 = (s32[1,2]{1,0:T(1,128)S(1)}, s32[1,2]{1,0:T(1,128)}, u32[]{:S(2)}) copy-start(s32[1,2]{1,0:T(1,128)} %kinds_ref.1) | copy-start | bytes 28
  47.3 3.9 %copy-start.4 = (s32[1,2]{1,0:T(1,128)S(1)}, s32[1,2]{1,0:T(1,128)}, u32[]{:S(2)}) copy-start(s32[1,2]{1,0:T(1,128)} %groups_ref.1) | copy-start | bytes 28
  49.2 2.0 %collective-permute-start.1 = (bf16[256,1152]{1,0:T(8,128)(2,1)S(1)}, bf16[256,1152]{1,0:T(8,128)(2,1)S(1)}, u32[]{:S(2)}, u32[]{:S(2)}) collective-permute-start(bf16[256,1152]{1,0:T(8,128)(2,1)S(1)} %get-tuple-element.17.own_ref), channel_id=1, source_target_pairs={{0,1},{1,0},{2,3},{3,2},{4,5},{5,4},{6,7},{7,6},{8,9},{9,8},{10,11... | collective-permute-start | bytes 1769480 | tf_op jit(solution)/shard_map/ppermute | solution.py:360

commit v10 on v9

--- a/solution.py
+++ b/solution.py
@@ -356,7 +356,6 @@
         name="observe",
     )(arrived, measured_point.reshape(1, tile), measured_reading.reshape(1, tile))
 
-    seen, other_noise = lax.optimization_barrier((seen, other_noise))
     other_seen = lax.ppermute(seen, "region", swap)
 
     own_gain, own_covariance = pl.pallas_call(

time: 92 us -> 92.3 us (level)
    ppermute x1, waiting for transfers between devices: 1.01 us -> 0.01 us  [shards(): other_seen = lax.ppermute(seen, 'region', swap)]
    ppermute x1, waiting for transfers between devices: 0.44 us -> 1.37 us  [shards(): other_noise = lax.ppermute(own_noise, 'region', swap)]
  transfers between devices with their start and end apart: 2 -> 2, of which waited for: 2 -> 1; matrix products, arithmetic and copies ran while one was open for 0% -> 0% of each run, Pallas kernels for 2% -> 1%
where the time goes in v10:
time: 92.3 us; the launch traced here: 92 us
  blocking collectives  77.3 us (84%)
  Pallas kernels  12.7 us (14%)
  waiting for transfers between devices  1.38 us (1%)
    all_to_all x2, blocking collectives, exchange(): lax.all_to_all(value, 'member', split_axis=0, concat_axis=0, axis_index_g...  77.3 us
    pallas_call x1, Pallas kernels, shards(): pl.pallas_call(analyse, in_specs=[pl.BlockSpec(memory_space=pltpu.SMEM)]...  4.97 us
    pallas_call x1, Pallas kernels, shards(): pl.pallas_call(pack_members, in_specs=[pl.BlockSpec(memory_space=pltpu.HB...  3.12 us
    pallas_call x1, Pallas kernels, shards(): pl.pallas_call(unpack_members, in_specs=[pl.BlockSpec(memory_space=pltpu....  2.29 us
  transfers between devices with their start and end apart: 2, of which 1 were waited for; matrix products, arithmetic and copies ran while one was open for 0% of the time, Pallas kernels for 1%

profile of v10, /device:TPU:0, one launch (start us, length us, event | category | flops | bytes accessed | tf_op | source)
XLA Modules:
  0.0 92.0 jit_solution(3470007643653962624)
XLA Ops:
  0.0 3.1 %pack_members.1 = bf16[64,16,1152]{2,1,0:T(8,128)(2,1)S(1)} custom-call(f32[16,64,8,128]{3,2,1,0:T(8,128)} %bitcast.9), custom_call_target="tpu_custom_call" | custom-call | flops 4194304 | bytes 7340032 | tf_op jit(solution)/shard_map/pack_members/pallas_call | solution.py:320
  3.1 0.0 copy-start.1
  3.1 0.0 copy-start.2
  3.2 44.0 %all_to_all.10.x_ref = bf16[64,16,1152]{2,1,0:T(8,128)(2,1)S(1)} all-to-all(bf16[64,16,1152]{2,1,0:T(8,128)(2,1)S(1)} %pack_members.1), channel_id=1, replica_groups={{0,42,84,126,40,82,124,38,80,122,36,78,120,34,76,118,32,74,116,30,72,11..., dimensions={0} | all-to-all | bytes 4718592 | tf_op jit(solution)/shard_map/all_to_all | solution.py:35
  47.1 0.0 copy-start
  47.1 0.0 copy-done.1
  47.1 0.0 copy-done.2
  47.1 0.0 copy-start.3
  47.1 0.0 copy-start.4
  47.1 1.4 %observe.1 = (bf16[1024,1024]{1,0:T(8,128)(2,1)S(1)}, bf16[256,1152]{1,0:T(8,128)(2,1)S(1)}) custom-call(bf16[64,16,1152]{2,1,0:T(8,128)(2,1)S(1)} %all_to_all.10.x_ref, s32[1,256]{1,0:T(1,128)S(1)} %bitcast.7, f32[1,256]{1,0:T(1,128)S(1)} %bitcast.8), custom_call_target="tpu_custom_call" | custom-call | flops 536870912 | bytes 8388608 | tf_op jit(solution)/shard_map/observe/pallas_call | solution.py:339
  48.6 0.1 collective-permute-start
  48.7 0.0 copy-done
  48.7 0.5 collective-permute-start.1
  49.2 0.9 own_part.1
  50.0 1.4 %collective-permute-done.1.other_noise_ref = bf16[256,1024]{1,0:T(8,128)(2,1)S(1)} collective-permute-done((bf16[256,1024]{1,0:T(8,128)(2,1)S(1)}, bf16[256,1024]{1,0:T(8,128)(2,1)S(1)}, u32[]{:S(2)}, u32[]{:S(2)}) %collective-permute-start.1) | collective-permute-done | bytes 524320 | tf_op jit(solution)/shard_map/ppermute | solution.py:337
  51.4 0.0 collective-permute-done.other_ref
  51.4 0.0 copy-done.3
  51.4 0.0 copy-done.4
  51.4 5.0 %analyse.1 = bf16[64,16,1024]{2,1,0:T(8,128)(2,1)S(1)} custom-call(s32[1,2]{1,0:T(1,128)S(1)} %copy-done.3, s32[1,2]{1,0:T(1,128)S(1)} %copy-done.4, bf16[1024,1024]{1,0:T(8,128)(2,1)S(1)} %get-tuple-element.12.anomaly_ref, bf16[256,1152]{1,0:T(8,128)(2,1)S(1)} %get-tuple-element.13.own_ref, bf16[256,1024]{1,0:T(8,128)(2,1)S(1)} %get-tuple-element.14.own_gain_ref, ...), custom_call_target="tpu_custom_call" | custom-call | tf_op jit(solution)/shard_map/analyse/pallas_call | solution.py:376
  56.4 33.3 %all_to_all.11.x_ref = bf16[64,16,1024]{2,1,0:T(8,128)(2,1)S(1)} all-to-all(bf16[64,16,1024]{2,1,0:T(8,128)(2,1)S(1)} %analyse.1), channel_id=1, replica_groups={{0,42,84,126,40,82,124,38,80,122,36,78,120,34,76,118,32,74,116,30,72,11..., dimensions={0} | all-to-all | bytes 4194304 | tf_op jit(solution)/shard_map/all_to_all | solution.py:35
  89.7 2.3 %unpack_members.1 = f32[16,64,8,128]{3,2,1,0:T(8,128)} custom-call(bf16[64,16,1024]{2,1,0:T(8,128)(2,1)S(1)} %all_to_all.11.x_ref), custom_call_target="tpu_custom_call" | custom-call | tf_op jit(solution)/shard_map/unpack_members/pallas_call | solution.py:407
Async XLA Ops:
  3.1 44.0 %copy-start.1 = (s32[1,1,256]{2,1,0:T(1,128)S(1)}, s32[1,1,256]{2,1,0:T(1,128)}, u32[]{:S(2)}) copy-start(s32[1,1,256]{2,1,0:T(1,128)} %param.7) | copy-start | bytes 3076
  3.1 44.0 %copy-start.2 = (f32[1,1,256]{2,1,0:T(1,128)S(1)}, f32[1,1,256]{2,1,0:T(1,128)}, u32[]{:S(2)}) copy-start(f32[1,1,256]{2,1,0:T(1,128)} %param.8) | copy-start | bytes 3076
  47.1 1.5 %copy-start = (bf16[1,1,256,1024]{3,2,1,0:T(8,128)(2,1)S(1)}, bf16[1,1,256,1024]{3,2,1,0:T(8,128)(2,1)}, u32[]{:S(2)}) copy-start(bf16[1,1,256,1024]{3,2,1,0:T(8,128)(2,1)} %param.9) | copy-start | bytes 1572868
  47.1 4.3 %copy-start.3 = (s32[1,2]{1,0:T(1,128)S(1)}, s32[1,2]{1,0:T(1,128)}, u32[]{:S(2)}) copy-start(s32[1,2]{1,0:T(1,128)} %kinds_ref.1) | copy-start | bytes 28
  47.1 4.3 %copy-start.4 = (s32[1,2]{1,0:T(1,128)S(1)}, s32[1,2]{1,0:T(1,128)}, u32[]{:S(2)}) copy-start(s32[1,2]{1,0:T(1,128)} %groups_ref.1) | copy-start | bytes 28
  48.6 2.8 %collective-permute-start = (bf16[256,1152]{1,0:T(8,128)(2,1)S(1)}, bf16[256,1152]{1,0:T(8,128)(2,1)S(1)}, u32[]{:S(2)}, u32[]{:S(2)}) collective-permute-start(bf16[256,1152]{1,0:T(8,128)(2,1)S(1)} %get-tuple-element.13.own_ref), channel_id=1, source_target_pairs={{0,1},{1,0},{2,3},{3,2},{4,5},{5,4},{6,7},{7,6},{8,9},{9,8},{10,11... | collective-permute-start | bytes 1769480 | tf_op jit(solution)/shard_map/ppermute | solution.py:359
  48.7 2.7 %collective-permute-start.1 = (bf16[256,1024]{1,0:T(8,128)(2,1)S(1)}, bf16[256,1024]{1,0:T(8,128)(2,1)S(1)}, u32[]{:S(2)}, u32[]{:S(2)}) collective-permute-start(bf16[256,1024]{1,0:T(8,128)(2,1)S(1)} %bitcast.5), channel_id=1, source_target_pairs={{0,1},{1,0},{2,3},{3,2},{4,5},{5,4},{6,7},{7,6},{8,9},{9,8},{10,11... | collective-permute-start | bytes 1572872 | tf_op jit(solution)/shard_map/ppermute | solution.py:337
